TPU v7x, 32 devices: a whole 2x2x4 slice. The times are simulated.
32 devices in a mesh: groups: 2 (over y), tensor: 2 (over x), expert: 4 (over z), dp: 2 (over core).
Axes of the slice: x: 2, y: 2, z: 4, core: 2. Of those that a mesh axis runs over, the one named last changes fastest.
Arguments:
- tokens: bfloat16 [1024, 6144], P(('groups', 'expert'), ('tensor', 'dp')), parts along dimension 0, may hold values from -6 to 6
- output_gradient: bfloat16 [1024, 6144], P(('groups', 'expert'), ('tensor', 'dp')), parts along dimension 0, may hold values from -6 to 6
- chosen_expert_index: int32 [1024, 2], P(('groups', 'expert')), parts along dimension 0, may hold values from 0 to 3, all different within a row; in each aligned block of 128 rows (0 to 127, 128 to 255, ...) at most 80 rows name the same one
- router_gate_weights: float32 [1024, 2], P(('groups', 'expert')), parts along dimension 0, may hold values from 0.1 to 0.9
- gate_frozen_weight: bfloat16 [4, 6144, 8192], P('expert', None, ('tensor', 'dp')), may hold values from -0.078125 to 0.078125
- up_frozen_weight: bfloat16 [4, 6144, 8192], P('expert', None, ('tensor', 'dp')), may hold values from -0.078125 to 0.078125
- down_frozen_weight: bfloat16 [4, 8192, 6144], P('expert', ('tensor', 'dp')), may hold values from -0.0625 to 0.0625
- gate_adapter_input: bfloat16 [4, 6144, 64], P('expert', ('tensor', 'dp')), may hold values from -0.078125 to 0.078125
- gate_adapter_output: bfloat16 [4, 64, 8192], P('expert', None, ('tensor', 'dp')), may hold values from -0.1796875 to 0.1796875
- up_adapter_input: bfloat16 [4, 6144, 64], P('expert', ('tensor', 'dp')), may hold values from -0.078125 to 0.078125
- up_adapter_output: bfloat16 [4, 64, 8192], P('expert', None, ('tensor', 'dp')), may hold values from -0.1796875 to 0.1796875
- down_adapter_input: bfloat16 [4, 8192, 64], P('expert', ('tensor', 'dp')), may hold values from -0.0625 to 0.0625
- down_adapter_output: bfloat16 [4, 64, 6144], P('expert', None, ('tensor', 'dp')), may hold values from -0.1796875 to 0.1796875
Outputs:
- mixed_out: bfloat16 [1024, 6144], P(('groups', 'expert'), ('tensor', 'dp')), parts along dimension 0
- grad_tokens: bfloat16 [1024, 6144], P(('groups', 'expert'), ('tensor', 'dp')), parts along dimension 0
- prob_grads: float32 [1024, 2], P(('groups', 'expert')), parts along dimension 0
- grad_gate_a: float32 [8, 6144, 64], P(('groups', 'expert'), ('tensor', 'dp')), parts along dimension 0
- grad_gate_b: float32 [8, 64, 8192], P(('groups', 'expert'), None, ('tensor', 'dp')), parts along dimension 0
- grad_up_a: float32 [8, 6144, 64], P(('groups', 'expert'), ('tensor', 'dp')), parts along dimension 0
- grad_up_b: float32 [8, 64, 8192], P(('groups', 'expert'), None, ('tensor', 'dp')), parts along dimension 0
- grad_down_a: float32 [8, 8192, 64], P(('groups', 'expert'), ('tensor', 'dp')), parts along dimension 0
- grad_down_b: float32 [8, 64, 6144], P(('groups', 'expert'), None, ('tensor', 'dp')), parts along dimension 0
There are 2 independent parts, one for each index of `groups`. A program takes and returns all parts, laid end to end along the dimension named above; an argument that names none is the same for every part. Nothing has to cross between parts.
Inputs may be any that keep to these rules, and one draw needn't show every extreme that they name: `chosen_expert_index`: each token names two different experts. Among the 128 tokens of one aligned block, no expert is named by more than 80 tokens, and in some block some expert is named by exactly 80.
All inputs are finite; a program needn't handle non-finite values.
Results may differ from a plain program's by a relative error of at most 0.007.
Values may be sent and summed in bfloat16 or wider, within the bound.
A program may use at most 256 MiB of HBM per device.

v0:
```python
import jax
import jax.numpy as jnp
from jax import lax
from jax.sharding import PartitionSpec as P

adapter_scale = 2.0


def contract_matrices(left_op, right_op, left_dim, right_dim):
    return lax.dot_general(
        left_op,
        right_op,
        (((left_dim,), (right_dim,)), ((), ())),
        preferred_element_type=jnp.float32,
    )


def silu_parts(gate_preactivation):
    sig_val = jax.nn.sigmoid(gate_preactivation)
    return (gate_preactivation * sig_val, sig_val * (1.0 + gate_preactivation * (1.0 - sig_val)))


def build_table(chosen_expert_index, experts, capacity):
    flat_ids = chosen_expert_index.reshape(-1)
    hit_mask = (flat_ids[:, None] == jnp.arange(experts, dtype=jnp.int32)[None, :]).astype(
        jnp.int32
    )
    before = jnp.cumsum(hit_mask, axis=0) - hit_mask
    slot_num = jnp.sum(before * hit_mask, axis=1)
    target = flat_ids * capacity + slot_num
    return (target[:, None] == jnp.arange(experts * capacity, dtype=jnp.int32)[None, :]).astype(
        jnp.bfloat16
    )


def collect(results, slot_map, experts, capacity):
    returned = lax.all_to_all(
        results.reshape(experts, capacity, -1), "expert", split_axis=0, concat_axis=0, tiled=True
    )
    return contract_matrices(slot_map, returned.reshape(experts * capacity, -1), 1, 0)


def expert_forward(
    input_full_rows,
    gate_weight_matrix,
    up_weight_matrix,
    gate_output_factor,
    up_output_factor,
    gate_rank_codes,
    up_rank_codes,
):
    gate_preactivation = contract_matrices(
        input_full_rows, gate_weight_matrix, 1, 0
    ) + adapter_scale * contract_matrices(gate_rank_codes, gate_output_factor, 1, 0)
    up_preactivation = contract_matrices(
        input_full_rows, up_weight_matrix, 1, 0
    ) + adapter_scale * contract_matrices(up_rank_codes, up_output_factor, 1, 0)
    silu_val, silu_grad = silu_parts(gate_preactivation)
    hidden_activation = (silu_val * up_preactivation).astype(jnp.bfloat16)
    return (up_preactivation, silu_val, silu_grad, hidden_activation)


def expert_backward(
    token_full_rows,
    backward_down_codes,
    down_weight_matrix,
    down_input_factor,
    gate_weight_matrix,
    up_weight_matrix,
    gate_output_factor,
    up_output_factor,
    up_preactivation,
    silu_val,
    silu_grad,
):
    hidden_gradient = contract_matrices(
        token_full_rows, down_weight_matrix, 1, 1
    ) + contract_matrices(backward_down_codes, down_input_factor, 1, 1)
    gate_preact_gradient = (hidden_gradient * up_preactivation * silu_grad).astype(jnp.bfloat16)
    up_preact_gradient = (hidden_gradient * silu_val).astype(jnp.bfloat16)
    dx_terms = contract_matrices(
        gate_preact_gradient, gate_weight_matrix, 1, 1
    ) + contract_matrices(up_preact_gradient, up_weight_matrix, 1, 1)
    code_terms = (
        contract_matrices(gate_preact_gradient, gate_output_factor, 1, 1),
        contract_matrices(up_preact_gradient, up_output_factor, 1, 1),
    )
    return (gate_preact_gradient, up_preact_gradient, dx_terms, code_terms)


def flat_sum(partial_terms, extra_term):
    main_sum = lax.psum_scatter(partial_terms, ("tensor", "dp"), scatter_dimension=1, tiled=True)
    return (main_sum + extra_term).astype(jnp.bfloat16)


def per_device(
    tokens,
    output_gradient,
    chosen_expert_index,
    router_gate_weights,
    gate_frozen_weight,
    up_frozen_weight,
    down_frozen_weight,
    gate_adapter_input,
    gate_adapter_output,
    up_adapter_input,
    up_adapter_output,
    down_adapter_input,
    down_adapter_output,
):
    experts = lax.axis_size("expert")
    tok_count = tokens.shape[0]
    capacity = max(5 * tok_count // 8, 2 * tok_count // experts)
    buffer_rows = experts * capacity
    slot_map = build_table(chosen_expert_index, experts, capacity)
    probs_flat = router_gate_weights.reshape(-1, 1)
    gate_weight_matrix = gate_frozen_weight[0]
    up_weight_matrix = up_frozen_weight[0]
    down_weight_matrix = down_frozen_weight[0]
    gate_input_factor = gate_adapter_input[0]
    gate_output_factor = gate_adapter_output[0]
    up_input_factor = up_adapter_input[0]
    up_output_factor = up_adapter_output[0]
    down_input_factor = down_adapter_input[0]
    down_output_factor = down_adapter_output[0]
    t_rows = (jnp.repeat(output_gradient, 2, axis=0).astype(jnp.float32) * probs_flat).astype(
        jnp.bfloat16
    )
    x_buf = (
        contract_matrices(slot_map, jnp.repeat(tokens, 2, axis=0), 0, 0)
        .astype(jnp.bfloat16)
        .reshape(experts, capacity, -1)
    )
    t_buf = (
        contract_matrices(slot_map, t_rows, 0, 0)
        .astype(jnp.bfloat16)
        .reshape(experts, capacity, -1)
    )
    x_arrived, t_arrived = (
        lax.all_to_all(x_buf, "expert", split_axis=0, concat_axis=0, tiled=True),
        lax.all_to_all(t_buf, "expert", split_axis=0, concat_axis=0, tiled=True),
    )
    x_part = x_arrived.reshape(buffer_rows, -1)
    token_partial_rows = t_arrived.reshape(buffer_rows, -1)
    rank_code_totals = lax.psum(
        (
            contract_matrices(x_part, gate_input_factor, 1, 0),
            contract_matrices(x_part, up_input_factor, 1, 0),
            contract_matrices(token_partial_rows, down_output_factor, 1, 1),
        ),
        ("tensor", "dp"),
    )
    gate_rank_codes = rank_code_totals[0].astype(jnp.bfloat16)
    up_rank_codes = rank_code_totals[1].astype(jnp.bfloat16)
    backward_down_codes = (adapter_scale * rank_code_totals[2]).astype(jnp.bfloat16)
    input_full_rows, token_full_rows = (
        lax.all_gather(x_part, ("tensor", "dp"), axis=1, tiled=True),
        lax.all_gather(token_partial_rows, ("tensor", "dp"), axis=1, tiled=True),
    )
    up_preactivation, silu_val, silu_grad, hidden_activation = expert_forward(
        input_full_rows,
        gate_weight_matrix,
        up_weight_matrix,
        gate_output_factor,
        up_output_factor,
        gate_rank_codes,
        up_rank_codes,
    )
    down_rank_codes = lax.psum(
        contract_matrices(hidden_activation, down_input_factor, 1, 0), ("tensor", "dp")
    ).astype(jnp.bfloat16)
    out_part = flat_sum(
        contract_matrices(hidden_activation, down_weight_matrix, 1, 0),
        adapter_scale * contract_matrices(down_rank_codes, down_output_factor, 1, 0),
    )
    gate_preact_gradient, up_preact_gradient, dx_terms, code_terms = expert_backward(
        token_full_rows,
        backward_down_codes,
        down_weight_matrix,
        down_input_factor,
        gate_weight_matrix,
        up_weight_matrix,
        gate_output_factor,
        up_output_factor,
        up_preactivation,
        silu_val,
        silu_grad,
    )
    backward_rank_codes = lax.psum((code_terms[0], code_terms[1]), ("tensor", "dp"))
    gate_code_gradient = (adapter_scale * backward_rank_codes[0]).astype(jnp.bfloat16)
    up_code_gradient = (adapter_scale * backward_rank_codes[1]).astype(jnp.bfloat16)
    dx_part = flat_sum(
        dx_terms,
        contract_matrices(gate_code_gradient, gate_input_factor, 1, 1)
        + contract_matrices(up_code_gradient, up_input_factor, 1, 1),
    )
    grad_list = (
        contract_matrices(x_part, gate_code_gradient, 0, 0),
        adapter_scale * contract_matrices(gate_rank_codes, gate_preact_gradient, 0, 0),
        contract_matrices(x_part, up_code_gradient, 0, 0),
        adapter_scale * contract_matrices(up_rank_codes, up_preact_gradient, 0, 0),
        contract_matrices(hidden_activation, backward_down_codes, 0, 0),
        adapter_scale * contract_matrices(down_rank_codes, token_partial_rows, 0, 0),
    )
    out_pairs = collect(out_part, slot_map, experts, capacity).reshape(tok_count, 2, -1)
    mixed_out = jnp.sum(out_pairs * router_gate_weights[:, :, None], axis=1).astype(jnp.bfloat16)
    prob_terms = jnp.sum(out_pairs * output_gradient[:, None, :].astype(jnp.float32), axis=2)
    prob_grads = lax.psum(prob_terms, ("tensor", "dp"))
    dx_pairs = collect(dx_part, slot_map, experts, capacity).reshape(tok_count, 2, -1)
    grad_tokens = jnp.sum(dx_pairs, axis=1).astype(jnp.bfloat16)
    return (
        mixed_out,
        grad_tokens,
        prob_grads,
        grad_list[0][None],
        grad_list[1][None],
        grad_list[2][None],
        grad_list[3][None],
        grad_list[4][None],
        grad_list[5][None],
    )


def solution(mesh):
    in_specs = (
        P(("groups", "expert"), ("tensor", "dp")),
        P(("groups", "expert"), ("tensor", "dp")),
        P(("groups", "expert"), None),
        P(("groups", "expert"), None),
        P("expert", None, ("tensor", "dp")),
        P("expert", None, ("tensor", "dp")),
        P("expert", ("tensor", "dp"), None),
        P("expert", ("tensor", "dp"), None),
        P("expert", None, ("tensor", "dp")),
        P("expert", ("tensor", "dp"), None),
        P("expert", None, ("tensor", "dp")),
        P("expert", ("tensor", "dp"), None),
        P("expert", None, ("tensor", "dp")),
    )
    out_specs = (
        P(("groups", "expert"), ("tensor", "dp")),
        P(("groups", "expert"), ("tensor", "dp")),
        P(("groups", "expert"), None),
        P(("groups", "expert"), ("tensor", "dp"), None),
        P(("groups", "expert"), None, ("tensor", "dp")),
        P(("groups", "expert"), ("tensor", "dp"), None),
        P(("groups", "expert"), None, ("tensor", "dp")),
        P(("groups", "expert"), ("tensor", "dp"), None),
        P(("groups", "expert"), None, ("tensor", "dp")),
    )
    return jax.shard_map(
        per_device, mesh=mesh, in_specs=in_specs, out_specs=out_specs, check_vma=False
    )
```

profile of v0, /device:TPU:0, one launch (start us, length us, event | category | flops | bytes accessed | tf_op | source)
XLA Modules:
  0.0 394.6 jit_solution(15212006535822921680)
XLA Ops:
  12.3 30.5 %all_to_all.20 = bf16[4,80,1536]{2,1,0:T(8,128)(2,1)} all-to-all(bf16[4,80,1536]{2,1,0:T(8,128)(2,1)S(1)} %bitcast.136), channel_id=1, replica_groups=mesh['groups'=2,'tensor'=2,'expert'=4,'dp'=2] {'expert'}, dimensions={0} | all-to-all | bytes 1966080 | tf_op jit(solution)/shard_map/all_to_all | solution.py:140
  47.9 27.1 %all_to_all.21 = bf16[4,80,1536]{2,1,0:T(8,128)(2,1)} all-to-all(bf16[4,80,1536]{2,1,0:T(8,128)(2,1)S(1)} %bitcast.135), channel_id=1, replica_groups=mesh['groups'=2,'tensor'=2,'expert'=4,'dp'=2] {'expert'}, dimensions={0} | all-to-all | bytes 1966080 | tf_op jit(solution)/shard_map/all_to_all | solution.py:141
  77.3 14.9 %all-reduce.9 = (bf16[320,64]{0,1:T(8,128)(2,1)S(1)}, bf16[320,64]{0,1:T(8,128)(2,1)}) all-reduce(f32[320,64]{0,1:T(8,128)S(1)} %fusion.43, f32[320,64]{0,1:T(8,128)S(1)} %fusion.47), channel_id=1, replica_groups=mesh['groups'=2,'tensor'=2,'expert'=4,'dp'=2] {'tensor','dp'}, use_global_device_ids=true, to_apply=%region_4.5 | all-reduce | flops 40960 | bytes 245760 | tf_op jit(solution)/shard_map/psum | solution.py:145
  92.2 18.7 %fusion.6 = f32[320,2048]{1,0:T(8,128)} fusion(bf16[320,6144]{1,0:T(8,128)(2,1)} %all-gather.3.cloned.1.call-done, bf16[1,6144,2048]{2,1,0:T(8,128)(2,1)} %param.18), kind=kOutput, calls=%fused_computation.6 | convolution fusion | flops 8053063680 | bytes 31719424 | tf_op jit(solution)/shard_map/dot_general | solution.py:10
  110.9 14.1 %fusion.10 = f32[320,2048]{1,0:T(8,128)} fusion(bf16[320,6144]{1,0:T(8,128)(2,1)S(1)} %copy-done.20, bf16[1,6144,2048]{2,1,0:T(8,128)(2,1)} %param.17), kind=kOutput, calls=%fused_computation.10 | convolution fusion | flops 8053063680 | bytes 31719424 | tf_op jit(solution)/shard_map/dot_general | solution.py:10
  125.1 15.4 %fusion = f32[320,2048]{1,0:T(8,128)} fusion(bf16[320,6144]{1,0:T(8,128)(2,1)} %all-gather.5.cloned.1.call-done, bf16[1,2048,6144]{2,1,0:T(8,128)(2,1)} %param.19), kind=kOutput, calls=%fused_computation | convolution fusion | flops 8053063680 | bytes 31719424 | tf_op jit(solution)/shard_map/dot_general | solution.py:10
  140.5 3.9 fusion.17
  147.8 3.3 multiply_convert_fusion.1
  151.1 15.4 %fusion.4 = f32[320,6144]{1,0:T(8,128)} fusion(bf16[320,2048]{1,0:T(8,128)(2,1)} %get-tuple-element.16, bf16[1,6144,2048]{2,1,0:T(8,128)(2,1)} %param.18), kind=kOutput, calls=%fused_computation.4 | convolution fusion | flops 8053063680 | bytes 34340864 | tf_op jit(solution)/shard_map/dot_general | solution.py:10
  171.5 17.9 %fusion.12 = f32[320,6144]{1,0:T(8,128)} fusion(f32[320,6144]{1,0:T(8,128)} %fusion.4, bf16[320,2048]{1,0:T(8,128)(2,1)} %get-tuple-element.15, bf16[1,6144,2048]{2,1,0:T(8,128)(2,1)} %param.17), kind=kOutput, calls=%fused_computation.12 | convolution fusion | flops 8055029760 | bytes 42205184 | tf_op jit(solution)/shard_map/dot_general | solution.py:10
  189.5 15.1 %fusion.2 = f32[320,6144]{1,0:T(8,128)} fusion(bf16[320,2048]{1,0:T(8,128)(2,1)S(1)} %get-tuple-element.17, bf16[1,2048,6144]{2,1,0:T(8,128)(2,1)} %param.19), kind=kOutput, calls=%fused_computation.2 | convolution fusion | flops 8053063680 | bytes 34340864 | tf_op jit(solution)/shard_map/dot_general | solution.py:10
  204.6 2.7 fusion.45
  207.3 67.4 %reduce-scatter.5.cloned.1.call-done = f32[320,1536]{1,0:T(8,128)} async-done(((f32[320,6144]{1,0:T(8,128)}), f32[320,1536]{1,0:T(8,128)}) %reduce-scatter.5.cloned.1.call-update) | async-done | bytes 1966096 | tf_op jit(solution)/shard_map/reduce_scatter | solution.py:92
  274.8 3.8 fusion.20
  278.6 4.6 %all-to-all-start.3 = ((bf16[4,80,1536]{2,1,0:T(8,128)(2,1)}), bf16[4,80,1536]{2,1,0:T(8,128)(2,1)}, u32[]{:S(2)}, u32[]{:S(2)}) async-start(bf16[4,80,1536]{2,1,0:T(8,128)(2,1)} %bitcast.133), calls=%async_computation.5 | async-start | bytes 1966080 | tf_op jit(solution)/shard_map/all_to_all | solution.py:37
  285.3 13.1 %psum.51 = bf16[320,64]{0,1:T(8,128)(2,1)} all-reduce(f32[320,64]{0,1:T(8,128)} %fusion.31), channel_id=1, replica_groups=mesh['groups'=2,'tensor'=2,'expert'=4,'dp'=2] {'tensor','dp'}, use_global_device_ids=true, to_apply=%region_6.7 | all-reduce | flops 20480 | bytes 122880 | tf_op jit(solution)/shard_map/psum | solution.py:169
  298.4 47.9 %reduce-scatter.3.cloned.1.call-done = f32[320,1536]{1,0:T(8,128)} async-done(((f32[320,6144]{1,0:T(8,128)}), f32[320,1536]{1,0:T(8,128)}) %reduce-scatter.3.cloned.1.call-update) | async-done | bytes 1966096 | tf_op jit(solution)/shard_map/reduce_scatter | solution.py:92
  346.4 3.1 fusion.19
  349.5 4.6 %all-to-all-start.1 = ((bf16[4,80,1536]{2,1,0:T(8,128)(2,1)}), bf16[4,80,1536]{2,1,0:T(8,128)(2,1)}, u32[]{:S(2)}, u32[]{:S(2)}) async-start(bf16[4,80,1536]{2,1,0:T(8,128)(2,1)} %bitcast.134), calls=%async_computation.2 | async-start | bytes 1966080 | tf_op jit(solution)/shard_map/all_to_all | solution.py:37
  359.7 2.6 fusion.23
  366.8 2.7 convolution_reduce_fusion
  369.4 9.1 %all-to-all-done.1 = bf16[4,80,1536]{2,1,0:T(8,128)(2,1)} async-done(((bf16[4,80,1536]{2,1,0:T(8,128)(2,1)}), bf16[4,80,1536]{2,1,0:T(8,128)(2,1)}, u32[]{:S(2)}, u32[]{:S(2)}) %all-to-all-start.1) | async-done | bytes 983072 | tf_op jit(solution)/shard_map/all_to_all | solution.py:37
  378.5 2.8 multiply_reduce_fusion
  381.3 6.4 %psum.55 = f32[128,2]{0,1:T(2,128)} all-reduce(f32[128,2]{0,1:T(2,128)S(1)} %get-tuple-element.9), channel_id=1, replica_groups=mesh['groups'=2,'tensor'=2,'expert'=4,'dp'=2] {'tensor','dp'}, use_global_device_ids=true, to_apply=%region_14.15 | all-reduce | flops 256 | bytes 2048 | tf_op jit(solution)/shard_map/psum | solution.py:208
  (98 shorter events, 33.2 us)
Async XLA Ops:
  7.2 139.7 %copy-start = (bf16[1,64,2048]{2,1,0:T(8,128)(2,1)S(1)}, bf16[1,64,2048]{2,1,0:T(8,128)(2,1)}, u32[]{:S(2)}) copy-start(bf16[1,64,2048]{2,1,0:T(8,128)(2,1)} %param.21) | copy-start | bytes 786436
  7.2 85.0 %all-gather.3.cloned.1.call-start = ((), (), s32[]{:S(2)}) async-start(), calls=%async_computation.6 | async-start | bytes 4915200 | tf_op jit(solution)/shard_map/all_gather | solution.py:157
  11.7 31.2 %copy-start.5 = (bf16[128,1536]{1,0:T(8,128)(2,1)S(1)}, bf16[128,1536]{1,0:T(8,128)(2,1)}, u32[]{:S(2)}) copy-start(bf16[128,1536]{1,0:T(8,128)(2,1)} %param.14) | copy-start | bytes 1179652
  42.9 82.2 %all-gather.5.cloned.1.call-start = ((), (), s32[]{:S(2)}) async-start(), calls=%async_computation.8 | async-start | bytes 4915200 | tf_op jit(solution)/shard_map/all_gather | solution.py:158
  45.8 29.2 %copy-start.1 = (bf16[4,80,1536]{2,1,0:T(8,128)(2,1)S(1)}, bf16[4,80,1536]{2,1,0:T(8,128)(2,1)}, u32[]{:S(2)}) copy-start(bf16[4,80,1536]{2,1,0:T(8,128)(2,1)} %all_to_all.20) | copy-start | bytes 2949124
  45.8 29.2 %copy-start.8 = (bf16[1,1536,64]{1,2,0:T(8,128)(2,1)S(1)}, bf16[1,1536,64]{1,2,0:T(8,128)(2,1)}, u32[]{:S(2)}) copy-start(bf16[1,1536,64]{1,2,0:T(8,128)(2,1)} %param.22) | copy-start | bytes 589828
  47.9 27.6 %copy-start.9 = (bf16[1,1536,64]{1,2,0:T(8,128)(2,1)S(1)}, bf16[1,1536,64]{1,2,0:T(8,128)(2,1)}, u32[]{:S(2)}) copy-start(bf16[1,1536,64]{1,2,0:T(8,128)(2,1)} %param.20) | copy-start | bytes 589828
  47.9 28.1 %copy-start.10 = (bf16[1,64,1536]{2,1,0:T(8,128)(2,1)S(1)}, bf16[1,64,1536]{2,1,0:T(8,128)(2,1)}, u32[]{:S(2)}) copy-start(bf16[1,64,1536]{2,1,0:T(8,128)(2,1)} %param.25) | copy-start | bytes 589828
  75.0 69.4 %all-reduce.6.cloned.1.call-start = ((), (), s32[]{:S(2)}) async-start(), calls=%async_computation.9 | async-start | bytes 196608 | tf_op jit(solution)/shard_map/psum | solution.py:145
  77.3 127.3 %all-reduce.8.cloned.1.call-start = ((), (), s32[]{:S(2)}) async-start(), calls=%async_computation.11 | async-start | bytes 393216 | tf_op jit(solution)/shard_map/psum | solution.py:189
  92.2 48.2 %copy-start.15 = (bf16[320,64]{0,1:T(8,128)(2,1)}, bf16[320,64]{0,1:T(8,128)(2,1)S(1)}, u32[]{:S(2)}) copy-start(bf16[320,64]{0,1:T(8,128)(2,1)S(1)} %get-tuple-element.11) | copy-start | bytes 122884
  92.2 18.7 %copy-start.20 = (bf16[320,6144]{1,0:T(8,128)(2,1)S(1)}, bf16[320,6144]{1,0:T(8,128)(2,1)}, u32[]{:S(2)}) copy-start(bf16[320,6144]{1,0:T(8,128)(2,1)} %all-gather.3.cloned.1.call-done) | copy-start | bytes 11796484
  125.0 15.4 %copy-start.7 = (bf16[1,64,2048]{2,1,0:T(8,128)(2,1)S(1)}, bf16[1,64,2048]{2,1,0:T(8,128)(2,1)}, u32[]{:S(2)}) copy-start(bf16[1,64,2048]{2,1,0:T(8,128)(2,1)} %param.23) | copy-start | bytes 786436
  140.5 4.0 %copy-start.6 = (bf16[1,2048,64]{1,2,0:T(8,128)(2,1)S(1)}, bf16[1,2048,64]{1,2,0:T(8,128)(2,1)}, u32[]{:S(2)}) copy-start(bf16[1,2048,64]{1,2,0:T(8,128)(2,1)} %param.24) | copy-start | bytes 786436
  171.4 103.4 %reduce-scatter.5.cloned.1.call-start = ((), (), s32[]{:S(2)}) async-start(), calls=%async_computation.10 | async-start | bytes 9830400 | tf_op jit(solution)/shard_map/reduce_scatter | solution.py:92
  189.4 156.9 %reduce-scatter.3.cloned.1.call-start = ((), (), s32[]{:S(2)}) async-start(), calls=%async_computation.7 | async-start | bytes 9830400 | tf_op jit(solution)/shard_map/reduce_scatter | solution.py:92
  278.6 70.9 %all-to-all-start.3 = ((bf16[4,80,1536]{2,1,0:T(8,128)(2,1)}), bf16[4,80,1536]{2,1,0:T(8,128)(2,1)}, u32[]{:S(2)}, u32[]{:S(2)}) async-start(bf16[4,80,1536]{2,1,0:T(8,128)(2,1)} %bitcast.133), calls=%async_computation.5 | async-start | bytes 1966080 | tf_op jit(solution)/shard_map/all_to_all | solution.py:37
  298.4 59.2 %copy-start.18 = (s32[128,2]{0,1:T(2,128)S(1)}, s32[128,2]{0,1:T(2,128)}, u32[]{:S(2)}) copy-start(s32[128,2]{0,1:T(2,128)} %param.15) | copy-start | bytes 3076
  349.5 29.0 %all-to-all-start.1 = ((bf16[4,80,1536]{2,1,0:T(8,128)(2,1)}), bf16[4,80,1536]{2,1,0:T(8,128)(2,1)}, u32[]{:S(2)}, u32[]{:S(2)}) async-start(bf16[4,80,1536]{2,1,0:T(8,128)(2,1)} %bitcast.134), calls=%async_computation.2 | async-start | bytes 1966080 | tf_op jit(solution)/shard_map/all_to_all | solution.py:37
  357.7 4.6 %copy-start.3 = (bf16[320,2048]{1,0:T(8,128)(2,1)S(1)}, bf16[320,2048]{1,0:T(8,128)(2,1)}, u32[]{:S(2)}) copy-start(bf16[320,2048]{1,0:T(8,128)(2,1)} %get-tuple-element.16) | copy-start | bytes 3932164
  357.7 4.6 %copy-start.16 = (bf16[320,64]{0,1:T(8,128)(2,1)S(1)}, bf16[320,64]{0,1:T(8,128)(2,1)}, u32[]{:S(2)}) copy-start(bf16[320,64]{0,1:T(8,128)(2,1)} %copy-done.15) | copy-start | bytes 122884
  357.7 5.8 %copy-start.14 = (f32[320,64]{0,1:T(8,128)S(1)}, f32[320,64]{0,1:T(8,128)}, u32[]{:S(2)}) copy-start(f32[320,64]{0,1:T(8,128)} %all-reduce.6.cloned.1.call-done) | copy-start | bytes 245764
  359.7 5.0 %copy-start.12 = (f32[320,64]{0,1:T(8,128)S(1)}, f32[320,64]{0,1:T(8,128)}, u32[]{:S(2)}) copy-start(f32[320,64]{0,1:T(8,128)} %get-tuple-element.13) | copy-start | bytes 245764
  364.7 13.9 %copy-start.11 = (f32[128,1536]{1,0:T(8,128)S(1)}, f32[128,1536]{1,0:T(8,128)}, u32[]{:S(2)}) copy-start(f32[128,1536]{1,0:T(8,128)} %convert_element_type.74) | copy-start | bytes 2359300
  (6 other events, 15.9 us)
Sparse Core Ops, SparseCore 0:
  43.0 32.0 all-gather.2
  76.7 34.0 all-gather.4
  113.6 30.7 all-reduce.5
  171.5 31.8 all-reduce.7
  205.8 68.9 reduce-scatter.4
  277.3 69.0 reduce-scatter.2
where the time goes:
time: 396 us; the launch traced here: 395 us
  matrix products  142 us (36%)
  waiting for transfers between devices  125 us (32%)
  blocking collectives  92.1 us (23%)
  between operations  14.4 us (4%)
  starting transfers between devices  9.45 us (2%)
  local copies, waits for them, and re-layouts  8.89 us (2%)
    dot_general x28, matrix products, contract_matrices(): lax.dot_general(left_op, right_op, (((left_dim,), (right_dim,)), ((), ())...  142 us
    reduce_scatter x2, waiting for transfers between devices, flat_sum(): lax.psum_scatter(partial_terms, ('tensor', 'dp'), scatter_dimension=1, ti...  115 us
    all_to_all x1, blocking collectives, per_device(): lax.all_to_all(x_buf, 'expert', split_axis=0, concat_axis=0, tiled=True)  30.5 us
    all_to_all x1, blocking collectives, per_device(): lax.all_to_all(t_buf, 'expert', split_axis=0, concat_axis=0, tiled=True)  27.1 us
    psum x1, blocking collectives, per_device(): lax.psum((contract_matrices(x_part, gate_input_factor, 1, 0), contract_ma...  14.9 us
    psum x1, blocking collectives, per_device(): lax.psum(contract_matrices(hidden_activation, down_input_factor, 1, 0), (...  13.1 us
    all_to_all x2, starting transfers between devices, collect(): lax.all_to_all(results.reshape(experts, capacity, -1), 'expert', split_ax...  9.21 us
    all_to_all x2, waiting for transfers between devices, collect(): lax.all_to_all(results.reshape(experts, capacity, -1), 'expert', split_ax...  9.07 us
  transfers between devices with their start and end apart: 8, of which 4 were waited for; matrix products, arithmetic and copies ran while one was open for 30% of the time, Pallas kernels for 0%

commit v1 on v0

--- a/solution.py
+++ b/solution.py
@@ -1,6 +1,8 @@
 import jax
 import jax.numpy as jnp
 from jax import lax
+from jax.experimental import pallas as pl
+from jax.experimental.pallas import tpu as pltpu
 from jax.sharding import PartitionSpec as P
 
 adapter_scale = 2.0
@@ -91,6 +93,283 @@
 def flat_sum(partial_terms, extra_term):
     main_sum = lax.psum_scatter(partial_terms, ("tensor", "dp"), scatter_dimension=1, tiled=True)
     return (main_sum + extra_term).astype(jnp.bfloat16)
+
+
+vmem_bytes = 48 * 1024 * 1024
+
+
+def nn(left_op, right_op):
+    return contract_matrices(left_op, right_op, 1, 0)
+
+
+def nt(left_op, right_op):
+    return contract_matrices(left_op, right_op, 1, 1)
+
+
+def call_tiles(body, tiles, order, operands, in_specs, out_shape, out_specs, flops, moved):
+    return pl.pallas_call(
+        body,
+        grid_spec=pltpu.PrefetchScalarGridSpec(
+            num_scalar_prefetch=1, grid=(tiles,), in_specs=in_specs, out_specs=out_specs
+        ),
+        out_shape=out_shape,
+        compiler_params=pltpu.CompilerParams(vmem_limit_bytes=vmem_bytes),
+        cost_estimate=pl.CostEstimate(flops=flops, bytes_accessed=moved, transcendentals=0),
+    )(order, *operands)
+
+
+def whole(arr):
+    return pl.BlockSpec(arr.shape, lambda n, order: (0, 0))
+
+
+def forward_tiles(order, pieces, gate_w, up_w, gate_codes, up_codes, gate_b, up_b, tile=256):
+    rows, width = pieces[0].shape
+    hidden = gate_w.shape[1]
+    parts = len(pieces)
+
+    def body(order_ref, *refs):
+        xs, gs, us = refs[:parts], refs[parts : 2 * parts], refs[2 * parts : 3 * parts]
+        gc, uc, gb, ub, hid_ref, up_ref, val_ref = refs[3 * parts :]
+        gate = adapter_scale * nn(gc[...], gb[...])
+        up = adapter_scale * nn(uc[...], ub[...])
+        for x_ref, g_ref in zip(xs, gs):
+            gate += nn(x_ref[...], g_ref[...])
+        for x_ref, u_ref in zip(xs, us):
+            up += nn(x_ref[...], u_ref[...])
+        val, grad = silu_parts(gate)
+        hid_ref[...] = (val * up).astype(jnp.bfloat16)
+        up_ref[...] = up * grad
+        val_ref[...] = val
+
+    def weight(k):
+        return pl.BlockSpec((width, tile), lambda n, order: (order[k], n))
+
+    def column(arr):
+        return pl.BlockSpec((arr.shape[0], tile), lambda n, order: (0, n))
+
+    out = pl.BlockSpec((rows, tile), lambda n, order: (0, n))
+    return call_tiles(
+        body,
+        hidden // tile,
+        order,
+        (*pieces, *[gate_w] * parts, *[up_w] * parts, gate_codes, up_codes, gate_b, up_b),
+        [whole(p) for p in pieces]
+        + [weight(k) for k in range(parts)] * 2
+        + [whole(gate_codes), whole(up_codes), column(gate_b), column(up_b)],
+        (
+            jax.ShapeDtypeStruct((rows, hidden), jnp.bfloat16),
+            jax.ShapeDtypeStruct((rows, hidden), jnp.float32),
+            jax.ShapeDtypeStruct((rows, hidden), jnp.float32),
+        ),
+        (out, out, out),
+        4 * rows * width * parts * hidden,
+        4 * width * parts * hidden,
+    )
+
+
+def backward_tiles(order, pieces, down_w, codes, down_a, up_term, silu_val, tile=256):
+    rows, width = pieces[0].shape
+    hidden = down_w.shape[0]
+    parts = len(pieces)
+
+    def body(order_ref, *refs):
+        ts, ws = refs[:parts], refs[parts : 2 * parts]
+        bc, da, up_ref, val_ref, dg_ref, du_ref = refs[2 * parts :]
+        grad = nt(bc[...], da[...])
+        for t_ref, w_ref in zip(ts, ws):
+            grad += nt(t_ref[...], w_ref[...])
+        dg_ref[...] = (grad * up_ref[...]).astype(jnp.bfloat16)
+        du_ref[...] = (grad * val_ref[...]).astype(jnp.bfloat16)
+
+    def weight(k):
+        return pl.BlockSpec((tile, width), lambda n, order: (n, order[k]))
+
+    out = pl.BlockSpec((rows, tile), lambda n, order: (0, n))
+    return call_tiles(
+        body,
+        hidden // tile,
+        order,
+        (*pieces, *[down_w] * parts, codes, down_a, up_term, silu_val),
+        [whole(p) for p in pieces]
+        + [weight(k) for k in range(parts)]
+        + [whole(codes), pl.BlockSpec((tile, down_a.shape[1]), lambda n, order: (n, 0)), out, out],
+        (jax.ShapeDtypeStruct((rows, hidden), jnp.bfloat16),) * 2,
+        (out, out),
+        2 * rows * width * parts * hidden,
+        2 * width * parts * hidden,
+    )
+
+
+def feature_piece(order, k, left, weights, transposed, width, added, kind, tile):
+    rows, hidden = left[0].shape
+    count = len(left)
+    steps = width // tile
+
+    def body(order_ref, *refs):
+        total = None
+        for l_ref, w_ref in zip(refs[:count], refs[count : 2 * count]):
+            term = (nt if transposed else nn)(l_ref[...], w_ref[...])
+            total = term if total is None else total + term
+        if added is not None:
+            total = total + refs[2 * count][...].astype(jnp.float32)
+        refs[-1][...] = total.astype(kind)
+
+    out = pl.BlockSpec((rows, tile), lambda n, order: (0, n))
+    if transposed:
+        weight = pl.BlockSpec((tile, hidden), lambda n, order: (order[k] * steps + n, 0))
+    else:
+        weight = pl.BlockSpec((hidden, tile), lambda n, order: (0, order[k] * steps + n))
+    extra = () if added is None else (added,)
+    return call_tiles(
+        body,
+        steps,
+        order,
+        (*left, *weights, *extra),
+        [whole(a) for a in left] + [weight] * count + [out] * len(extra),
+        jax.ShapeDtypeStruct((rows, width), kind),
+        out,
+        2 * rows * hidden * width * count,
+        2 * hidden * width * count,
+    )
+
+
+def swap(arr, axis):
+    return lax.ppermute(arr, axis, [(0, 1), (1, 0)])
+
+
+def sum_pairs(arr):
+    arr = arr + swap(arr, "dp")
+    return arr + swap(arr, "tensor")
+
+
+def rotate(arr, shift, experts):
+    if shift % experts == 0:
+        return arr
+    return lax.ppermute(arr, "expert", [(e, (e + shift) % experts) for e in range(experts)])
+
+
+def quad_device(
+    tokens,
+    output_gradient,
+    chosen_expert_index,
+    router_gate_weights,
+    gate_frozen_weight,
+    up_frozen_weight,
+    down_frozen_weight,
+    gate_adapter_input,
+    gate_adapter_output,
+    up_adapter_input,
+    up_adapter_output,
+    down_adapter_input,
+    down_adapter_output,
+):
+    experts = lax.axis_size("expert")
+    me = lax.axis_index("expert")
+    tok_count, width = tokens.shape
+    capacity = max(5 * tok_count // 8, 2 * tok_count // experts)
+    buffer_rows = experts * capacity
+    far, near = lax.axis_index("tensor"), lax.axis_index("dp")
+    order = jnp.stack(
+        [2 * far + near, 2 * far + 1 - near, 2 * (1 - far) + near, 2 * (1 - far) + 1 - near]
+    ).astype(jnp.int32)
+    gate_w, up_w, down_w = gate_frozen_weight[0], up_frozen_weight[0], down_frozen_weight[0]
+    gate_a, up_a, down_a = gate_adapter_input[0], up_adapter_input[0], down_adapter_input[0]
+    gate_b, up_b, down_b = gate_adapter_output[0], up_adapter_output[0], down_adapter_output[0]
+
+    hits = [
+        chosen_expert_index[:, k : k + 1] == jnp.arange(experts, dtype=jnp.int32)[None, :]
+        for k in range(2)
+    ]
+    both = (hits[0] | hits[1]).astype(jnp.bfloat16)
+    place = jnp.arange(tok_count, dtype=jnp.int32)
+    earlier = (place[:, None] > place[None, :]).astype(jnp.bfloat16)
+    before = nn(earlier, both).astype(jnp.int32)
+    slot_maps = []
+    for k in range(2):
+        slot_num = jnp.sum(jnp.where(hits[k], before, 0), axis=1)
+        turned = lax.rem(chosen_expert_index[:, k] - me + experts, experts)
+        target = turned * capacity + slot_num
+        slot_maps.append(
+            (target[:, None] == jnp.arange(buffer_rows, dtype=jnp.int32)[None, :]).astype(
+                jnp.bfloat16
+            )
+        )
+    token_map = slot_maps[0] + slot_maps[1]
+    gradient_wide = output_gradient.astype(jnp.float32)
+    probs = [router_gate_weights[:, k : k + 1] for k in range(2)]
+
+    def dispatch(buf):
+        cut = [buf[s * capacity : (s + 1) * capacity] for s in range(experts)]
+        own = [rotate(cut[s], s, experts) for s in range(experts)]
+        other = [swap(block, "tensor") for block in own]
+        own, other = jnp.concatenate(own), jnp.concatenate(other)
+        return (own, swap(own, "dp"), other, swap(other, "dp"))
+
+    x_buf = contract_matrices(token_map, tokens, 0, 0).astype(jnp.bfloat16)
+    t_buf = (
+        contract_matrices(slot_maps[0], (gradient_wide * probs[0]).astype(jnp.bfloat16), 0, 0)
+        + contract_matrices(slot_maps[1], (gradient_wide * probs[1]).astype(jnp.bfloat16), 0, 0)
+    ).astype(jnp.bfloat16)
+    x_pieces = dispatch(x_buf)
+    t_pieces = dispatch(t_buf)
+    x_part, t_part = x_pieces[0], t_pieces[0]
+    codes = sum_pairs(nn(x_part, jnp.concatenate([gate_a, up_a], axis=1))).astype(jnp.bfloat16)
+    rank = gate_a.shape[1]
+    gate_codes, up_codes = codes[:, :rank], codes[:, rank:]
+    back_down = (adapter_scale * sum_pairs(nt(t_part, down_b))).astype(jnp.bfloat16)
+
+    hidden_act, up_term, silu_val = forward_tiles(
+        order, x_pieces, gate_w, up_w, gate_codes, up_codes, gate_b, up_b
+    )
+
+    def scatter_sum(left, weights, transposed, tile):
+        def piece(k, added, kind):
+            return feature_piece(order, k, left, weights, transposed, width, added, kind, tile)
+
+        to_both = swap(piece(3, None, jnp.bfloat16), "dp")
+        to_core = swap(piece(1, None, jnp.bfloat16), "dp")
+        to_chip = piece(2, to_both, jnp.bfloat16)
+        kept = piece(0, to_core, jnp.float32)
+        return kept, to_chip
+
+    def send_back(kept, to_chip, extra):
+        sequence = [2 % experts] + [s for s in range(experts - 1, 0, -1) if s != 2] + [0]
+        arrived = {}
+        for s in dict.fromkeys(sequence):
+            cut = slice(s * capacity, (s + 1) * capacity)
+            block = (kept[cut] + extra[cut] + swap(to_chip[cut], "tensor").astype(jnp.float32))
+            arrived[s] = rotate(block.astype(jnp.bfloat16), -s, experts)
+        return jnp.concatenate([arrived[s] for s in range(experts)])
+
+    out_kept, out_chip = scatter_sum((hidden_act,), (down_w,), False, 512)
+    down_codes = sum_pairs(nn(hidden_act, down_a)).astype(jnp.bfloat16)
+    out_back = send_back(out_kept, out_chip, adapter_scale * nn(down_codes, down_b))
+
+    d_gate, d_up = backward_tiles(order, t_pieces, down_w, back_down, down_a, up_term, silu_val)
+    dx_kept, dx_chip = scatter_sum((d_gate, d_up), (gate_w, up_w), True, 256)
+    back_codes = adapter_scale * sum_pairs(
+        jnp.concatenate([nt(d_gate, gate_b), nt(d_up, up_b)], axis=1)
+    )
+    back_codes = back_codes.astype(jnp.bfloat16)
+    back_gate, back_up = back_codes[:, :rank], back_codes[:, rank:]
+    dx_back = send_back(dx_kept, dx_chip, nt(back_gate, gate_a) + nt(back_up, up_a))
+
+    grad_codes = contract_matrices(x_part, back_codes, 0, 0)
+    grad_list = (
+        grad_codes[:, :rank],
+        adapter_scale * contract_matrices(gate_codes, d_gate, 0, 0),
+        grad_codes[:, rank:],
+        adapter_scale * contract_matrices(up_codes, d_up, 0, 0),
+        contract_matrices(hidden_act, back_down, 0, 0),
+        adapter_scale * contract_matrices(down_codes, t_part, 0, 0),
+    )
+    rows_out = [nn(slot_maps[k], out_back) for k in range(2)]
+    mixed_out = (rows_out[0] * probs[0] + rows_out[1] * probs[1]).astype(jnp.bfloat16)
+    prob_grads = sum_pairs(
+        jnp.stack([jnp.sum(rows_out[k] * gradient_wide, axis=1) for k in range(2)], axis=1)
+    )
+    grad_tokens = nn(token_map, dx_back).astype(jnp.bfloat16)
+    return (mixed_out, grad_tokens, prob_grads, *[g[None] for g in grad_list])
 
 
 def per_device(
@@ -248,6 +527,7 @@
         P(("groups", "expert"), ("tensor", "dp"), None),
         P(("groups", "expert"), None, ("tensor", "dp")),
     )
+    quad = mesh.shape["tensor"] == 2 and mesh.shape["dp"] == 2
     return jax.shard_map(
-        per_device, mesh=mesh, in_specs=in_specs, out_specs=out_specs, check_vma=False
-    )
+        quad_device if quad else per_device, mesh=mesh, in_specs=in_specs, out_specs=out_specs, check_vma=False
+    )

time: 396 us -> 274 us (0.69)
  matrix products: 142 us -> 16.9 us
  Pallas kernels: 0 us -> 101 us
  blocking collectives: 92.1 us -> 0 us
  starting transfers between devices: 9.45 us -> 81.7 us
  waiting for transfers between devices: 125 us -> 63.6 us
  between operations: 14.4 us -> 1.33 us
    dot_general x28 -> x20, matrix products: 142 us -> 16.9 us  [contract_matrices(): lax.dot_general(left_op, right_op, (((left_dim,), (right_dim,)), ((), ())...]
    reduce_scatter x2 -> x0, waiting for transfers between devices: 115 us -> none  [flat_sum(): lax.psum_scatter(partial_terms, ('tensor', 'dp'), scatter_dimension=1, ti...]
    pallas_call x0 -> x10, Pallas kernels: none -> 101 us  [call_tiles(): pl.pallas_call(body, grid_spec=pltpu.PrefetchScalarGridSpec(num_scalar_pr...]
    ppermute x0 -> x46, starting transfers between devices: none -> 81.7 us  [the longest x12 53.1 us: rotate(): lax.ppermute(arr, 'expert', [(e, (e + shift) % experts) for e in range(ex...]
    ppermute x0 -> x46, waiting for transfers between devices: none -> 63.6 us  [the longest x34 41.7 us: swap(): return lax.ppermute(arr, axis, [(0, 1), (1, 0)])]
    all_to_all x2 -> x0, blocking collectives: 57.6 us -> none  [the longest x1 30.5 us: per_device(): lax.all_to_all(x_buf, 'expert', split_axis=0, concat_axis=0, tiled=True)]
    psum x3 -> x0, blocking collectives: 34.5 us -> none  [the longest x1 14.9 us: per_device(): lax.psum((contract_matrices(x_part, gate_input_factor, 1, 0), contract_ma...]
    all_to_all x2 -> x0, starting transfers between devices: 9.21 us -> none  [collect(): lax.all_to_all(results.reshape(experts, capacity, -1), 'expert', split_ax...]
  transfers between devices with their start and end apart: 8 -> 46, of which waited for: 4 -> 17; matrix products, arithmetic and copies ran while one was open for 30% -> 6% of each run, Pallas kernels for 0% -> 24%
where the time goes in v1:
time: 274 us; the launch traced here: 273 us
  Pallas kernels  101 us (37%)
  starting transfers between devices  81.7 us (30%)
  waiting for transfers between devices  63.6 us (23%)
  matrix products  16.9 us (6%)
  local copies, waits for them, and re-layouts  5.49 us (2%)
  other arithmetic  2.75 us (1%)
    pallas_call x10, Pallas kernels, call_tiles(): pl.pallas_call(body, grid_spec=pltpu.PrefetchScalarGridSpec(num_scalar_pr...  101 us
    ppermute x12, starting transfers between devices, rotate(): lax.ppermute(arr, 'expert', [(e, (e + shift) % experts) for e in range(ex...  53.1 us
    ppermute x34, waiting for transfers between devices, swap(): return lax.ppermute(arr, axis, [(0, 1), (1, 0)])  41.7 us
    ppermute x34, starting transfers between devices, swap(): return lax.ppermute(arr, axis, [(0, 1), (1, 0)])  28.6 us
    ppermute x12, waiting for transfers between devices, rotate(): lax.ppermute(arr, 'expert', [(e, (e + shift) % experts) for e in range(ex...  22 us
    dot_general x20, matrix products, contract_matrices(): lax.dot_general(left_op, right_op, (((left_dim,), (right_dim,)), ((), ())...  16.9 us
  transfers between devices with their start and end apart: 46, of which 17 were waited for; matrix products, arithmetic and copies ran while one was open for 6% of the time, Pallas kernels for 24%

profile of v1, /device:TPU:0, one launch (start us, length us, event | category | flops | bytes accessed | tf_op | source)
XLA Modules:
  0.0 272.8 jit_solution(9587355442076943841)
XLA Ops:
  16.0 11.5 %collective-permute-start.23 = (bf16[80,1536]{1,0:T(8,128)(2,1)S(1)}, bf16[80,1536]{1,0:T(8,128)(2,1)S(1)}, u32[]{:S(2)}, u32[]{:S(2)}) collective-permute-start(bf16[80,1536]{1,0:T(8,128)(2,1)S(1)} %get-tuple-element.38), channel_id=1, source_target_pairs={{0,4},{2,6},{4,0},{6,2},{1,5},{3,7},{5,1},{7,3},{8,12},{10,14},{12... | collective-permute-start | bytes 737288 | tf_op jit(solution)/shard_map/ppermute | solution.py:248
  27.5 14.1 %collective-permute-start.24 = (bf16[80,1536]{1,0:T(8,128)(2,1)S(1)}, bf16[80,1536]{1,0:T(8,128)(2,1)S(1)}, u32[]{:S(2)}, u32[]{:S(2)}) collective-permute-start(bf16[80,1536]{1,0:T(8,128)(2,1)S(1)} %get-tuple-element.37), channel_id=1, source_target_pairs={{0,6},{2,0},{4,2},{6,4},{1,7},{3,1},{5,3},{7,5},{8,14},{10,8},{12,... | collective-permute-start | bytes 737288 | tf_op jit(solution)/shard_map/ppermute | solution.py:248
  53.3 9.4 %collective-permute-done.32 = f32[320,64]{1,0:T(8,128)S(1)} collective-permute-done((f32[320,64]{1,0:T(8,128)S(1)}, f32[320,64]{1,0:T(8,128)S(1)}, u32[]{:S(2)}, u32[]{:S(2)}) %collective-permute-start.32) | collective-permute-done | bytes 81952 | tf_op jit(solution)/shard_map/ppermute | solution.py:237
  66.5 5.1 %collective-permute-done.6 = bf16[80,1536]{1,0:T(8,128)(2,1)S(1)} collective-permute-done((bf16[80,1536]{1,0:T(8,128)(2,1)S(1)}, bf16[80,1536]{1,0:T(8,128)(2,1)S(1)}, u32[]{:S(2)}, u32[]{:S(2)}) %collective-permute-start.6) | collective-permute-done | bytes 245792 | tf_op jit(solution)/shard_map/ppermute | solution.py:237
  73.1 3.8 %collective-permute-done.7 = bf16[80,1536]{1,0:T(8,128)(2,1)S(1)} collective-permute-done((bf16[80,1536]{1,0:T(8,128)(2,1)S(1)}, bf16[80,1536]{1,0:T(8,128)(2,1)S(1)}, u32[]{:S(2)}, u32[]{:S(2)}) %collective-permute-start.7) | collective-permute-done | bytes 245792 | tf_op jit(solution)/shard_map/ppermute | solution.py:237
  78.4 3.8 %collective-permute-done.27 = bf16[80,1536]{1,0:T(8,128)(2,1)S(1)} collective-permute-done((bf16[80,1536]{1,0:T(8,128)(2,1)S(1)}, bf16[80,1536]{1,0:T(8,128)(2,1)S(1)}, u32[]{:S(2)}, u32[]{:S(2)}) %collective-permute-start.27) | collective-permute-done | bytes 245792 | tf_op jit(solution)/shard_map/ppermute | solution.py:237
  82.1 5.2 %collective-permute-done.28 = bf16[80,1536]{1,0:T(8,128)(2,1)S(1)} collective-permute-done((bf16[80,1536]{1,0:T(8,128)(2,1)S(1)}, bf16[80,1536]{1,0:T(8,128)(2,1)S(1)}, u32[]{:S(2)}, u32[]{:S(2)}) %collective-permute-start.28) | collective-permute-done | bytes 245792 | tf_op jit(solution)/shard_map/ppermute | solution.py:237
  88.9 3.8 %collective-permute-done.29 = bf16[80,1536]{1,0:T(8,128)(2,1)S(1)} collective-permute-done((bf16[80,1536]{1,0:T(8,128)(2,1)S(1)}, bf16[80,1536]{1,0:T(8,128)(2,1)S(1)}, u32[]{:S(2)}, u32[]{:S(2)}) %collective-permute-start.29) | collective-permute-done | bytes 245792 | tf_op jit(solution)/shard_map/ppermute | solution.py:237
  94.6 26.1 %shard_map.196 = (bf16[320,2048]{1,0:T(8,128)(2,1)S(1)}, f32[320,2048]{1,0:T(8,128)}, f32[320,2048]{1,0:T(8,128)}) custom-call(s32[4]{0:T(128)S(1)} %pad_add_fusion.order_ref, bf16[320,1536]{1,0:T(8,128)(2,1)S(1)} %pad_maximum_fusion.refs_0_, bf16[320,1536]{1,0:T(8,128)(2,1)S(1)} %collective-permute-done.3.refs_1_, ...), custom_call_target="tpu_custom_call" | custom-call | flops 16106127360 | bytes 50331648 | tf_op jit(solution)/shard_map/pallas_call | solution.py:110
  120.7 5.5 %shard_map.199 = bf16[320,1536]{1,0:T(8,128)(2,1)S(1)} custom-call(s32[4]{0:T(128)S(1)} %pad_add_fusion.order_ref, bf16[320,2048]{1,0:T(8,128)(2,1)S(1)} %get-tuple-element.14.refs_0_, bf16[2048,6144]{1,0:T(8,128)(2,1)} %bitcast.80), custom_call_target="tpu_custom_call" | custom-call | flops 2013265920 | bytes 6291456 | tf_op jit(solution)/shard_map/pallas_call | solution.py:110
  126.1 5.5 %shard_map.197 = bf16[320,1536]{1,0:T(8,128)(2,1)S(1)} custom-call(s32[4]{0:T(128)S(1)} %pad_add_fusion.order_ref, bf16[320,2048]{1,0:T(8,128)(2,1)S(1)} %get-tuple-element.14.refs_0_, bf16[2048,6144]{1,0:T(8,128)(2,1)} %bitcast.81), custom_call_target="tpu_custom_call" | custom-call | flops 2013265920 | bytes 6291456 | tf_op jit(solution)/shard_map/pallas_call | solution.py:110
  132.1 16.4 %shard_map.201 = (bf16[320,2048]{1,0:T(8,128)(2,1)S(1)}, bf16[320,2048]{1,0:T(8,128)(2,1)}) custom-call(s32[4]{0:T(128)S(1)} %pad_add_fusion.order_ref, bf16[320,1536]{1,0:T(8,128)(2,1)S(1)} %pad_maximum_fusion.2.refs_0_, bf16[320,1536]{1,0:T(8,128)(2,1)S(1)} %collective-permute-done.25.refs_1_, ...), custom_call_target="tpu_custom_call" | custom-call | flops 8053063680 | bytes 25165824 | tf_op jit(solution)/shard_map/pallas_call | solution.py:110
  149.9 9.1 %shard_map.204 = bf16[320,1536]{1,0:T(8,128)(2,1)S(1)} custom-call(s32[4]{0:T(128)S(1)} %pad_add_fusion.order_ref, bf16[320,2048]{1,0:T(8,128)(2,1)S(1)} %get-tuple-element.17.refs_0_, bf16[320,2048]{1,0:T(8,128)(2,1)S(1)} %copy-done.2, bf16[6144,2048]{1,0:T(8,128)(2,1)} %bitcast.92, bf16[6144,2048]{1,0:T(8,128)(2,1)} %bitcast.100), custom_call_target="tpu_custom_call" | custom-call | flops 4026531840 | bytes 12582912 | tf_op jit(solution)/shard_map/pallas_call | solution.py:110
  158.9 9.1 %shard_map.202 = bf16[320,1536]{1,0:T(8,128)(2,1)S(1)} custom-call(s32[4]{0:T(128)S(1)} %pad_add_fusion.order_ref, bf16[320,2048]{1,0:T(8,128)(2,1)S(1)} %get-tuple-element.17.refs_0_, bf16[320,2048]{1,0:T(8,128)(2,1)S(1)} %copy-done.2, bf16[6144,2048]{1,0:T(8,128)(2,1)} %bitcast.93, bf16[6144,2048]{1,0:T(8,128)(2,1)} %bitcast.101), custom_call_target="tpu_custom_call" | custom-call | flops 4026531840 | bytes 12582912 | tf_op jit(solution)/shard_map/pallas_call | solution.py:110
  176.0 3.2 %collective-permute-done.13 = f32[320,64]{0,1:T(8,128)S(1)} collective-permute-done((f32[320,64]{0,1:T(8,128)S(1)}, f32[320,64]{0,1:T(8,128)S(1)}, u32[]{:S(2)}, u32[]{:S(2)}) %collective-permute-start.13) | collective-permute-done | bytes 81952 | tf_op jit(solution)/shard_map/ppermute | solution.py:237
  187.8 5.5 %shard_map.200 = bf16[320,1536]{1,0:T(8,128)(2,1)S(1)} custom-call(s32[4]{0:T(128)S(1)} %pad_add_fusion.order_ref, bf16[320,2048]{1,0:T(8,128)(2,1)S(1)} %get-tuple-element.14.refs_0_, bf16[2048,6144]{1,0:T(8,128)(2,1)} %bitcast.86, bf16[320,1536]{1,0:T(8,128)(2,1)S(1)} %collective-permute-done.14.refs_2_), custom_call_target="tpu_custom_call" | custom-call | flops 2013265920 | bytes 6291456 | tf_op jit(solution)/shard_map/pallas_call | solution.py:110
  197.0 9.1 %shard_map.205 = bf16[320,1536]{1,0:T(8,128)(2,1)S(1)} custom-call(s32[4]{0:T(128)S(1)} %pad_add_fusion.order_ref, bf16[320,2048]{1,0:T(8,128)(2,1)S(1)} %get-tuple-element.17.refs_0_, bf16[320,2048]{1,0:T(8,128)(2,1)S(1)} %copy-done.3, bf16[6144,2048]{1,0:T(8,128)(2,1)} %bitcast.94, bf16[6144,2048]{1,0:T(8,128)(2,1)} %bitcast.102, ...), custom_call_target="tpu_custom_call" | custom-call | flops 4026531840 | bytes 12582912 | tf_op jit(solution)/shard_map/pallas_call | solution.py:110
  206.8 9.1 %shard_map.203 = f32[320,1536]{1,0:T(8,128)S(1)} custom-call(s32[4]{0:T(128)S(1)} %pad_add_fusion.order_ref, bf16[320,2048]{1,0:T(8,128)(2,1)S(1)} %get-tuple-element.17.refs_0_, bf16[320,2048]{1,0:T(8,128)(2,1)S(1)} %copy-done.3, bf16[6144,2048]{1,0:T(8,128)(2,1)} %bitcast.95, bf16[6144,2048]{1,0:T(8,128)(2,1)} %bitcast.103, ...), custom_call_target="tpu_custom_call" | custom-call | flops 4026531840 | bytes 12582912 | tf_op jit(solution)/shard_map/pallas_call | solution.py:110
  217.5 5.7 %shard_map.198 = f32[320,1536]{1,0:T(8,128)S(1)} custom-call(s32[4]{0:T(128)S(1)} %pad_add_fusion.order_ref, bf16[320,2048]{1,0:T(8,128)(2,1)S(1)} %get-tuple-element.14.refs_0_, bf16[2048,6144]{1,0:T(8,128)(2,1)} %bitcast.87, bf16[320,1536]{1,0:T(8,128)(2,1)S(1)} %collective-permute-done.11.refs_2_), custom_call_target="tpu_custom_call" | custom-call | flops 2013265920 | bytes 6291456 | tf_op jit(solution)/shard_map/pallas_call | solution.py:110
  226.4 6.0 %collective-permute-start.17 = (bf16[80,1536]{1,0:T(8,128)(2,1)S(1)}, bf16[80,1536]{1,0:T(8,128)(2,1)S(1)}, u32[]{:S(2)}, u32[]{:S(2)}) collective-permute-start(bf16[80,1536]{1,0:T(8,128)(2,1)S(1)} %get-tuple-element.30), channel_id=1, source_target_pairs={{0,6},{2,0},{4,2},{6,4},{1,7},{3,1},{5,3},{7,5},{8,14},{10,8},{12,... | collective-permute-start | bytes 737288 | tf_op jit(solution)/shard_map/ppermute | solution.py:248
  232.4 4.1 %collective-permute-start.21 = (bf16[80,1536]{1,0:T(8,128)(2,1)S(1)}, bf16[80,1536]{1,0:T(8,128)(2,1)S(1)}, u32[]{:S(2)}, u32[]{:S(2)}) collective-permute-start(bf16[80,1536]{1,0:T(8,128)(2,1)S(1)} %get-tuple-element.28), channel_id=1, source_target_pairs={{0,2},{2,4},{4,6},{6,0},{1,3},{3,5},{5,7},{7,1},{8,10},{10,12},{12... | collective-permute-start | bytes 737288 | tf_op jit(solution)/shard_map/ppermute | solution.py:248
  239.1 6.0 %collective-permute-start.39 = (bf16[80,1536]{1,0:T(8,128)(2,1)S(1)}, bf16[80,1536]{1,0:T(8,128)(2,1)S(1)}, u32[]{:S(2)}, u32[]{:S(2)}) collective-permute-start(bf16[80,1536]{1,0:T(8,128)(2,1)S(1)} %get-tuple-element.26), channel_id=1, source_target_pairs={{0,6},{2,0},{4,2},{6,4},{1,7},{3,1},{5,3},{7,5},{8,14},{10,8},{12,... | collective-permute-start | bytes 737288 | tf_op jit(solution)/shard_map/ppermute | solution.py:248
  245.1 3.9 %collective-permute-start.43 = (bf16[80,1536]{1,0:T(8,128)(2,1)S(1)}, bf16[80,1536]{1,0:T(8,128)(2,1)S(1)}, u32[]{:S(2)}, u32[]{:S(2)}) collective-permute-start(bf16[80,1536]{1,0:T(8,128)(2,1)S(1)} %get-tuple-element.24), channel_id=1, source_target_pairs={{0,2},{2,4},{4,6},{6,0},{1,3},{3,5},{5,7},{7,1},{8,10},{10,12},{12... | collective-permute-start | bytes 737288 | tf_op jit(solution)/shard_map/ppermute | solution.py:248
  249.0 14.6 %collective-permute-done.19 = bf16[80,1536]{1,0:T(8,128)(2,1)S(1)} collective-permute-done((bf16[80,1536]{1,0:T(8,128)(2,1)S(1)}, bf16[80,1536]{1,0:T(8,128)(2,1)S(1)}, u32[]{:S(2)}, u32[]{:S(2)}) %collective-permute-start.19) | collective-permute-done | bytes 245792 | tf_op jit(solution)/shard_map/ppermute | solution.py:248
  (179 shorter events, 76.2 us)
Async XLA Ops:
  6.8 20.6 %collective-permute-start.1 = (bf16[80,1536]{1,0:T(8,128)(2,1)}, bf16[80,1536]{1,0:T(8,128)(2,1)S(1)}, u32[]{:S(2)}, u32[]{:S(2)}) collective-permute-start(bf16[80,1536]{1,0:T(8,128)(2,1)} %get-tuple-element.46), channel_id=1, source_target_pairs={{0,4},{2,6},{4,0},{6,2},{1,5},{3,7},{5,1},{7,3},{8,12},{10,14},{12... | collective-permute-start | bytes 737288 | tf_op jit(solution)/shard_map/ppermute | solution.py:248
  9.4 32.1 %collective-permute-start.2 = (bf16[80,1536]{1,0:T(8,128)(2,1)S(1)}, bf16[80,1536]{1,0:T(8,128)(2,1)S(1)}, u32[]{:S(2)}, u32[]{:S(2)}) collective-permute-start(bf16[80,1536]{1,0:T(8,128)(2,1)S(1)} %get-tuple-element.45), channel_id=1, source_target_pairs={{0,6},{2,0},{4,2},{6,4},{1,7},{3,1},{5,3},{7,5},{8,14},{10,8},{12,... | collective-permute-start | bytes 737288 | tf_op jit(solution)/shard_map/ppermute | solution.py:248
  10.8 38.1 %collective-permute-start.4 = (bf16[80,1536]{1,0:T(8,128)(2,1)S(1)}, bf16[80,1536]{1,0:T(8,128)(2,1)S(1)}, u32[]{:S(2)}, u32[]{:S(2)}) collective-permute-start(bf16[80,1536]{1,0:T(8,128)(2,1)S(1)} %get-tuple-element.44), channel_id=1, source_target_pairs={{0,8},{8,0},{1,9},{9,1},{2,10},{10,2},{3,11},{11,3},{4,12},{12,4},... | collective-permute-start | bytes 737288 | tf_op jit(solution)/shard_map/ppermute | solution.py:237
  14.2 30.4 %collective-permute-start.22 = (bf16[80,1536]{1,0:T(8,128)(2,1)}, bf16[80,1536]{1,0:T(8,128)(2,1)S(1)}, u32[]{:S(2)}, u32[]{:S(2)}) collective-permute-start(bf16[80,1536]{1,0:T(8,128)(2,1)} %get-tuple-element.39), channel_id=1, source_target_pairs={{0,2},{2,4},{4,6},{6,0},{1,3},{3,5},{5,7},{7,1},{8,10},{10,12},{12... | collective-permute-start | bytes 737288 | tf_op jit(solution)/shard_map/ppermute | solution.py:248
  16.0 30.8 %collective-permute-start.23 = (bf16[80,1536]{1,0:T(8,128)(2,1)S(1)}, bf16[80,1536]{1,0:T(8,128)(2,1)S(1)}, u32[]{:S(2)}, u32[]{:S(2)}) collective-permute-start(bf16[80,1536]{1,0:T(8,128)(2,1)S(1)} %get-tuple-element.38), channel_id=1, source_target_pairs={{0,4},{2,6},{4,0},{6,2},{1,5},{3,7},{5,1},{7,3},{8,12},{10,14},{12... | collective-permute-start | bytes 737288 | tf_op jit(solution)/shard_map/ppermute | solution.py:248
  27.5 20.8 %collective-permute-start.24 = (bf16[80,1536]{1,0:T(8,128)(2,1)S(1)}, bf16[80,1536]{1,0:T(8,128)(2,1)S(1)}, u32[]{:S(2)}, u32[]{:S(2)}) collective-permute-start(bf16[80,1536]{1,0:T(8,128)(2,1)S(1)} %get-tuple-element.37), channel_id=1, source_target_pairs={{0,6},{2,0},{4,2},{6,4},{1,7},{3,1},{5,3},{7,5},{8,14},{10,8},{12,... | collective-permute-start | bytes 737288 | tf_op jit(solution)/shard_map/ppermute | solution.py:248
  44.6 50.0 %collective-permute-start.3 = (bf16[320,1536]{1,0:T(8,128)(2,1)S(1)}, bf16[320,1536]{1,0:T(8,128)(2,1)S(1)}, u32[]{:S(2)}, u32[]{:S(2)}) collective-permute-start(bf16[320,1536]{1,0:T(8,128)(2,1)S(1)} %pad_maximum_fusion.refs_0_), channel_id=1, source_target_pairs={{0,1},{1,0},{2,3},{3,2},{4,5},{5,4},{6,7},{7,6},{8,9},{9,8},{10,11... | collective-permute-start | bytes 2949128 | tf_op jit(solution)/shard_map/ppermute | solution.py:237
  46.8 17.4 %collective-permute-start.9 = (f32[320,128]{1,0:T(8,128)S(1)}, f32[320,128]{1,0:T(8,128)S(1)}, u32[]{:S(2)}, u32[]{:S(2)}) collective-permute-start(f32[320,128]{1,0:T(8,128)S(1)} %fusion.34), channel_id=1, source_target_pairs={{0,1},{1,0},{2,3},{3,2},{4,5},{5,4},{6,7},{7,6},{8,9},{9,8},{10,11... | collective-permute-start | bytes 491528 | tf_op jit(solution)/shard_map/ppermute | solution.py:237
  48.3 83.8 %collective-permute-start.25 = (bf16[320,1536]{1,0:T(8,128)(2,1)S(1)}, bf16[320,1536]{1,0:T(8,128)(2,1)S(1)}, u32[]{:S(2)}, u32[]{:S(2)}) collective-permute-start(bf16[320,1536]{1,0:T(8,128)(2,1)S(1)} %pad_maximum_fusion.2.refs_0_), channel_id=1, source_target_pairs={{0,1},{1,0},{2,3},{3,2},{4,5},{5,4},{6,7},{7,6},{8,9},{9,8},{10,11... | collective-permute-start | bytes 2949128 | tf_op jit(solution)/shard_map/ppermute | solution.py:237
  64.9 17.2 %collective-permute-start.27 = (bf16[80,1536]{1,0:T(8,128)(2,1)S(1)}, bf16[80,1536]{1,0:T(8,128)(2,1)S(1)}, u32[]{:S(2)}, u32[]{:S(2)}) collective-permute-start(bf16[80,1536]{1,0:T(8,128)(2,1)S(1)} %collective-permute-done.22), channel_id=1, source_target_pairs={{0,8},{8,0},{1,9},{9,1},{2,10},{10,2},{3,11},{11,3},{4,12},{12,4},... | collective-permute-start | bytes 737288 | tf_op jit(solution)/shard_map/ppermute | solution.py:237
  92.7 39.5 %collective-permute-start.30 = (bf16[320,1536]{1,0:T(8,128)(2,1)S(1)}, bf16[320,1536]{1,0:T(8,128)(2,1)S(1)}, u32[]{:S(2)}, u32[]{:S(2)}) collective-permute-start(bf16[320,1536]{1,0:T(8,128)(2,1)S(1)} %constant_dynamic-update-slice_fusion.4.refs_2_), channel_id=1, source_target_pairs={{0,1},{1,0},{2,3},{3,2},{4,5},{5,4},{6,7},{7,6},{8,9},{9,8},{10,11... | collective-permute-start | bytes 2949128 | tf_op jit(solution)/shard_map/ppermute | solution.py:237
  173.3 42.6 %collective-permute-start.11 = (bf16[320,1536]{1,0:T(8,128)(2,1)S(1)}, bf16[320,1536]{1,0:T(8,128)(2,1)S(1)}, u32[]{:S(2)}, u32[]{:S(2)}) collective-permute-start(bf16[320,1536]{1,0:T(8,128)(2,1)S(1)} %shard_map.197), channel_id=1, source_target_pairs={{0,1},{1,0},{2,3},{3,2},{4,5},{5,4},{6,7},{7,6},{8,9},{9,8},{10,11... | collective-permute-start | bytes 2949128 | tf_op jit(solution)/shard_map/ppermute | solution.py:237
  173.8 21.7 %collective-permute-start.36 = (bf16[320,1536]{1,0:T(8,128)(2,1)S(1)}, bf16[320,1536]{1,0:T(8,128)(2,1)S(1)}, u32[]{:S(2)}, u32[]{:S(2)}) collective-permute-start(bf16[320,1536]{1,0:T(8,128)(2,1)S(1)} %shard_map.204), channel_id=1, source_target_pairs={{0,1},{1,0},{2,3},{3,2},{4,5},{5,4},{6,7},{7,6},{8,9},{9,8},{10,11... | collective-permute-start | bytes 2949128 | tf_op jit(solution)/shard_map/ppermute | solution.py:237
  173.9 32.3 %collective-permute-start.33 = (bf16[320,1536]{1,0:T(8,128)(2,1)S(1)}, bf16[320,1536]{1,0:T(8,128)(2,1)S(1)}, u32[]{:S(2)}, u32[]{:S(2)}) collective-permute-start(bf16[320,1536]{1,0:T(8,128)(2,1)S(1)} %shard_map.202), channel_id=1, source_target_pairs={{0,1},{1,0},{2,3},{3,2},{4,5},{5,4},{6,7},{7,6},{8,9},{9,8},{10,11... | collective-permute-start | bytes 2949128 | tf_op jit(solution)/shard_map/ppermute | solution.py:237
  193.4 29.8 %collective-permute-start.15 = (bf16[80,1536]{1,0:T(8,128)(2,1)S(1)}, bf16[80,1536]{1,0:T(8,128)(2,1)S(1)}, u32[]{:S(2)}, u32[]{:S(2)}) collective-permute-start(bf16[80,1536]{1,0:T(8,128)(2,1)S(1)} %get-tuple-element.40), channel_id=1, source_target_pairs={{0,8},{8,0},{1,9},{9,1},{2,10},{10,2},{3,11},{11,3},{4,12},{12,4},... | collective-permute-start | bytes 737288 | tf_op jit(solution)/shard_map/ppermute | solution.py:237
  195.0 28.9 %collective-permute-start.16 = (bf16[80,1536]{1,0:T(8,128)(2,1)S(1)}, bf16[80,1536]{1,0:T(8,128)(2,1)S(1)}, u32[]{:S(2)}, u32[]{:S(2)}) collective-permute-start(bf16[80,1536]{1,0:T(8,128)(2,1)S(1)} %get-tuple-element.43), channel_id=1, source_target_pairs={{0,8},{8,0},{1,9},{9,1},{2,10},{10,2},{3,11},{11,3},{4,12},{12,4},... | collective-permute-start | bytes 737288 | tf_op jit(solution)/shard_map/ppermute | solution.py:237
  195.5 29.8 %collective-permute-start.18 = (bf16[80,1536]{1,0:T(8,128)(2,1)S(1)}, bf16[80,1536]{1,0:T(8,128)(2,1)S(1)}, u32[]{:S(2)}, u32[]{:S(2)}) collective-permute-start(bf16[80,1536]{1,0:T(8,128)(2,1)S(1)} %get-tuple-element.42), channel_id=1, source_target_pairs={{0,8},{8,0},{1,9},{9,1},{2,10},{10,2},{3,11},{11,3},{4,12},{12,4},... | collective-permute-start | bytes 737288 | tf_op jit(solution)/shard_map/ppermute | solution.py:237
  206.2 19.7 %collective-permute-start.20 = (bf16[80,1536]{1,0:T(8,128)(2,1)S(1)}, bf16[80,1536]{1,0:T(8,128)(2,1)S(1)}, u32[]{:S(2)}, u32[]{:S(2)}) collective-permute-start(bf16[80,1536]{1,0:T(8,128)(2,1)S(1)} %get-tuple-element.41), channel_id=1, source_target_pairs={{0,8},{8,0},{1,9},{9,1},{2,10},{10,2},{3,11},{11,3},{4,12},{12,4},... | collective-permute-start | bytes 737288 | tf_op jit(solution)/shard_map/ppermute | solution.py:237
  226.4 18.7 %collective-permute-start.17 = (bf16[80,1536]{1,0:T(8,128)(2,1)S(1)}, bf16[80,1536]{1,0:T(8,128)(2,1)S(1)}, u32[]{:S(2)}, u32[]{:S(2)}) collective-permute-start(bf16[80,1536]{1,0:T(8,128)(2,1)S(1)} %get-tuple-element.30), channel_id=1, source_target_pairs={{0,6},{2,0},{4,2},{6,4},{1,7},{3,1},{5,3},{7,5},{8,14},{10,8},{12,... | collective-permute-start | bytes 737288 | tf_op jit(solution)/shard_map/ppermute | solution.py:248
  232.4 31.2 %collective-permute-start.19 = (bf16[80,1536]{1,0:T(8,128)(2,1)S(1)}, bf16[80,1536]{1,0:T(8,128)(2,1)S(1)}, u32[]{:S(2)}, u32[]{:S(2)}) collective-permute-start(bf16[80,1536]{1,0:T(8,128)(2,1)S(1)} %get-tuple-element.29), channel_id=1, source_target_pairs={{0,4},{2,6},{4,0},{6,2},{1,5},{3,7},{5,1},{7,3},{8,12},{10,14},{12... | collective-permute-start | bytes 737288 | tf_op jit(solution)/shard_map/ppermute | solution.py:248
  232.4 31.2 %collective-permute-start.21 = (bf16[80,1536]{1,0:T(8,128)(2,1)S(1)}, bf16[80,1536]{1,0:T(8,128)(2,1)S(1)}, u32[]{:S(2)}, u32[]{:S(2)}) collective-permute-start(bf16[80,1536]{1,0:T(8,128)(2,1)S(1)} %get-tuple-element.28), channel_id=1, source_target_pairs={{0,2},{2,4},{4,6},{6,0},{1,3},{3,5},{5,7},{7,1},{8,10},{10,12},{12... | collective-permute-start | bytes 737288 | tf_op jit(solution)/shard_map/ppermute | solution.py:248
  239.1 29.0 %collective-permute-start.39 = (bf16[80,1536]{1,0:T(8,128)(2,1)S(1)}, bf16[80,1536]{1,0:T(8,128)(2,1)S(1)}, u32[]{:S(2)}, u32[]{:S(2)}) collective-permute-start(bf16[80,1536]{1,0:T(8,128)(2,1)S(1)} %get-tuple-element.26), channel_id=1, source_target_pairs={{0,6},{2,0},{4,2},{6,4},{1,7},{3,1},{5,3},{7,5},{8,14},{10,8},{12,... | collective-permute-start | bytes 737288 | tf_op jit(solution)/shard_map/ppermute | solution.py:248
  245.1 26.0 %collective-permute-start.41 = (bf16[80,1536]{1,0:T(8,128)(2,1)S(1)}, bf16[80,1536]{1,0:T(8,128)(2,1)S(1)}, u32[]{:S(2)}, u32[]{:S(2)}) collective-permute-start(bf16[80,1536]{1,0:T(8,128)(2,1)S(1)} %get-tuple-element.25), channel_id=1, source_target_pairs={{0,4},{2,6},{4,0},{6,2},{1,5},{3,7},{5,1},{7,3},{8,12},{10,14},{12... | collective-permute-start | bytes 737288 | tf_op jit(solution)/shard_map/ppermute | solution.py:248
  245.1 26.0 %collective-permute-start.43 = (bf16[80,1536]{1,0:T(8,128)(2,1)S(1)}, bf16[80,1536]{1,0:T(8,128)(2,1)S(1)}, u32[]{:S(2)}, u32[]{:S(2)}) collective-permute-start(bf16[80,1536]{1,0:T(8,128)(2,1)S(1)} %get-tuple-element.24), channel_id=1, source_target_pairs={{0,2},{2,4},{4,6},{6,0},{1,3},{3,5},{5,7},{7,1},{8,10},{10,12},{12... | collective-permute-start | bytes 737288 | tf_op jit(solution)/shard_map/ppermute | solution.py:248
  (45 other events, 495.4 us)

commit v2 on v1

--- a/solution.py
+++ b/solution.py
@@ -106,13 +106,23 @@
     return contract_matrices(left_op, right_op, 1, 1)
 
 
-def call_tiles(body, tiles, order, operands, in_specs, out_shape, out_specs, flops, moved):
+def call_tiles(
+    body, tiles, order, operands, in_specs, out_shape, out_specs, flops, moved, after=(), alias=0
+):
+    count, extra = len(operands), len(after)
+    operands = (*operands, *after)
+    in_specs = [*in_specs, *[pl.BlockSpec(memory_space=pl.ANY)] * extra]
+
+    def inner(order_ref, *refs):
+        body(order_ref, *refs[:count], *refs[count + extra :])
+
     return pl.pallas_call(
-        body,
+        inner,
         grid_spec=pltpu.PrefetchScalarGridSpec(
             num_scalar_prefetch=1, grid=(tiles,), in_specs=in_specs, out_specs=out_specs
         ),
         out_shape=out_shape,
+        input_output_aliases={1 + count + a: a for a in range(alias)},
         compiler_params=pltpu.CompilerParams(vmem_limit_bytes=vmem_bytes),
         cost_estimate=pl.CostEstimate(flops=flops, bytes_accessed=moved, transcendentals=0),
     )(order, *operands)
@@ -122,10 +132,14 @@
     return pl.BlockSpec(arr.shape, lambda n, order: (0, 0))
 
 
-def forward_tiles(order, pieces, gate_w, up_w, gate_codes, up_codes, gate_b, up_b, tile=256):
+def forward_tiles(
+    order, pieces, gate_w, up_w, gate_codes, up_codes, gate_b, up_b, half, prior=(), after=(), tile=256
+):
     rows, width = pieces[0].shape
     hidden = gate_w.shape[1]
     parts = len(pieces)
+    steps = hidden // tile // 2
+    base = half * steps
 
     def body(order_ref, *refs):
         xs, gs, us = refs[:parts], refs[parts : 2 * parts], refs[2 * parts : 3 * parts]
@@ -142,15 +156,15 @@
         val_ref[...] = val
 
     def weight(k):
-        return pl.BlockSpec((width, tile), lambda n, order: (order[k], n))
+        return pl.BlockSpec((width, tile), lambda n, order: (order[k], base + n))
 
     def column(arr):
-        return pl.BlockSpec((arr.shape[0], tile), lambda n, order: (0, n))
-
-    out = pl.BlockSpec((rows, tile), lambda n, order: (0, n))
+        return pl.BlockSpec((arr.shape[0], tile), lambda n, order: (0, base + n))
+
+    out = pl.BlockSpec((rows, tile), lambda n, order: (0, base + n))
     return call_tiles(
         body,
-        hidden // tile,
+        steps,
         order,
         (*pieces, *[gate_w] * parts, *[up_w] * parts, gate_codes, up_codes, gate_b, up_b),
         [whole(p) for p in pieces]
@@ -162,12 +176,14 @@
             jax.ShapeDtypeStruct((rows, hidden), jnp.float32),
         ),
         (out, out, out),
-        4 * rows * width * parts * hidden,
-        4 * width * parts * hidden,
-    )
-
-
-def backward_tiles(order, pieces, down_w, codes, down_a, up_term, silu_val, tile=256):
+        2 * rows * width * parts * hidden,
+        2 * width * parts * hidden,
+        (*prior, *after),
+        len(prior),
+    )
+
+
+def backward_tiles(order, pieces, down_w, codes, down_a, up_term, silu_val, after=(), tile=256):
     rows, width = pieces[0].shape
     hidden = down_w.shape[0]
     parts = len(pieces)
@@ -197,10 +213,11 @@
         (out, out),
         2 * rows * width * parts * hidden,
         2 * width * parts * hidden,
-    )
-
-
-def feature_piece(order, k, left, weights, transposed, width, added, kind, tile):
+        after,
+    )
+
+
+def feature_piece(order, k, left, weights, transposed, width, added, kind, tile, after):
     rows, hidden = left[0].shape
     count = len(left)
     steps = width // tile
@@ -230,6 +247,49 @@
         out,
         2 * rows * hidden * width * count,
         2 * hidden * width * count,
+        after,
+    )
+
+
+def stack_rows(blocks, order, after):
+    height, width = blocks[0].shape
+
+    def body(order_ref, *refs):
+        for b, ref in enumerate(refs[:-1]):
+            refs[-1][b * height : (b + 1) * height, :] = ref[...]
+
+    shape = (height * len(blocks), width)
+    return call_tiles(
+        body,
+        1,
+        order,
+        blocks,
+        [whole(b) for b in blocks],
+        jax.ShapeDtypeStruct(shape, blocks[0].dtype),
+        pl.BlockSpec(shape, lambda n, order: (0, 0)),
+        0,
+        4 * shape[0] * width,
+        after,
+    )
+
+
+def add_block(kept, extra, met, s, order, after):
+    def body(order_ref, kept_ref, extra_ref, met_ref, out_ref):
+        total = kept_ref[...] + extra_ref[...] + met_ref[...].astype(jnp.float32)
+        out_ref[...] = total.astype(jnp.bfloat16)
+
+    rows = pl.BlockSpec(met.shape, lambda n, order: (s, 0))
+    return call_tiles(
+        body,
+        1,
+        order,
+        (kept, extra, met),
+        [rows, rows, whole(met)],
+        jax.ShapeDtypeStruct(met.shape, jnp.bfloat16),
+        whole(met),
+        0,
+        12 * met.shape[0] * met.shape[1],
+        after,
     )
 
 
@@ -298,61 +358,82 @@
     gradient_wide = output_gradient.astype(jnp.float32)
     probs = [router_gate_weights[:, k : k + 1] for k in range(2)]
 
-    def dispatch(buf):
+    def to_experts(buf):
         cut = [buf[s * capacity : (s + 1) * capacity] for s in range(experts)]
-        own = [rotate(cut[s], s, experts) for s in range(experts)]
-        other = [swap(block, "tensor") for block in own]
-        own, other = jnp.concatenate(own), jnp.concatenate(other)
-        return (own, swap(own, "dp"), other, swap(other, "dp"))
+        return [rotate(cut[s], s, experts) for s in range(experts)]
+
+    def across(blocks):
+        return jnp.concatenate([swap(block, "tensor") for block in blocks])
+
+    rank = gate_a.shape[1]
+    code_factor = jnp.concatenate([gate_a, up_a], axis=1)
+    code_far = swap(code_factor, "tensor")
+    code_factors = (code_factor, swap(code_factor, "dp"), code_far, swap(code_far, "dp"))
 
     x_buf = contract_matrices(token_map, tokens, 0, 0).astype(jnp.bfloat16)
     t_buf = (
         contract_matrices(slot_maps[0], (gradient_wide * probs[0]).astype(jnp.bfloat16), 0, 0)
         + contract_matrices(slot_maps[1], (gradient_wide * probs[1]).astype(jnp.bfloat16), 0, 0)
     ).astype(jnp.bfloat16)
-    x_pieces = dispatch(x_buf)
-    t_pieces = dispatch(t_buf)
-    x_part, t_part = x_pieces[0], t_pieces[0]
-    codes = sum_pairs(nn(x_part, jnp.concatenate([gate_a, up_a], axis=1))).astype(jnp.bfloat16)
-    rank = gate_a.shape[1]
+    x_blocks = to_experts(x_buf)
+    x_part, x_far = jnp.concatenate(x_blocks), across(x_blocks)
+    x_pieces = (x_part, swap(x_part, "dp"), x_far, swap(x_far, "dp"))
+    t_blocks = to_experts(stack_rows((t_buf,), order, x_blocks))
+
+    codes = sum(nn(x, a) for x, a in zip(x_pieces, code_factors)).astype(jnp.bfloat16)
     gate_codes, up_codes = codes[:, :rank], codes[:, rank:]
+
+    forward_args = (order, x_pieces, gate_w, up_w, gate_codes, up_codes, gate_b, up_b)
+    first_half = forward_tiles(*forward_args, 0)
+    t_part = stack_rows(t_blocks, order, first_half[:1])
+    t_far = across([t_part[s * capacity : (s + 1) * capacity] for s in range(experts)])
+    t_pieces = (t_part, swap(t_part, "dp"), t_far, swap(t_far, "dp"))
     back_down = (adapter_scale * sum_pairs(nt(t_part, down_b))).astype(jnp.bfloat16)
-
-    hidden_act, up_term, silu_val = forward_tiles(
-        order, x_pieces, gate_w, up_w, gate_codes, up_codes, gate_b, up_b
-    )
-
-    def scatter_sum(left, weights, transposed, tile):
-        def piece(k, added, kind):
-            return feature_piece(order, k, left, weights, transposed, width, added, kind, tile)
-
-        to_both = swap(piece(3, None, jnp.bfloat16), "dp")
-        to_core = swap(piece(1, None, jnp.bfloat16), "dp")
-        to_chip = piece(2, to_both, jnp.bfloat16)
-        kept = piece(0, to_core, jnp.float32)
-        return kept, to_chip
-
-    def send_back(kept, to_chip, extra):
-        sequence = [2 % experts] + [s for s in range(experts - 1, 0, -1) if s != 2] + [0]
+    hidden_act, up_term, silu_val = forward_tiles(*forward_args, 1, first_half, (t_part,))
+
+    def out_piece(k, added, kind, after):
+        return feature_piece(order, k, (hidden_act,), (down_w,), False, width, added, kind, 512, after)
+
+    def meet(to_chip):
+        return [
+            swap(to_chip[s * capacity : (s + 1) * capacity], "tensor") for s in range(experts)
+        ]
+
+    def send_back(kept, met, extra, gate):
         arrived = {}
-        for s in dict.fromkeys(sequence):
-            cut = slice(s * capacity, (s + 1) * capacity)
-            block = (kept[cut] + extra[cut] + swap(to_chip[cut], "tensor").astype(jnp.float32))
-            arrived[s] = rotate(block.astype(jnp.bfloat16), -s, experts)
-        return jnp.concatenate([arrived[s] for s in range(experts)])
-
-    out_kept, out_chip = scatter_sum((hidden_act,), (down_w,), False, 512)
+        for s in [*range(2, experts), 1, 0]:
+            gate = add_block(kept, extra, met[s], s, order, (gate,))
+            arrived[s] = rotate(gate, -s, experts)
+        return [arrived[s] for s in range(experts)]
+
+    out_3 = out_piece(3, None, jnp.bfloat16, (t_far,))
+    out_1 = out_piece(1, None, jnp.bfloat16, (out_3,))
     down_codes = sum_pairs(nn(hidden_act, down_a)).astype(jnp.bfloat16)
-    out_back = send_back(out_kept, out_chip, adapter_scale * nn(down_codes, down_b))
-
-    d_gate, d_up = backward_tiles(order, t_pieces, down_w, back_down, down_a, up_term, silu_val)
-    dx_kept, dx_chip = scatter_sum((d_gate, d_up), (gate_w, up_w), True, 256)
+    d_gate, d_up = backward_tiles(
+        order, t_pieces, down_w, back_down, down_a, up_term, silu_val, (out_1,)
+    )
+    out_chip = out_piece(2, swap(out_3, "dp"), jnp.bfloat16, (d_gate,))
+    out_kept = out_piece(0, swap(out_1, "dp"), jnp.float32, (out_chip,))
+    out_met = meet(out_chip)
+
+    def dx_piece(k, added, kind, after):
+        return feature_piece(
+            order, k, (d_gate, d_up), (gate_w, up_w), True, width, added, kind, 256, after
+        )
+
+    dx_3 = dx_piece(3, None, jnp.bfloat16, (out_kept,))
+    dx_1 = dx_piece(1, None, jnp.bfloat16, (dx_3,))
+    dx_chip = dx_piece(2, swap(dx_3, "dp"), jnp.bfloat16, (dx_1, *out_met))
+    out_back = send_back(out_kept, out_met, adapter_scale * nn(down_codes, down_b), dx_3)
+    dx_kept = dx_piece(0, swap(dx_1, "dp"), jnp.float32, (dx_chip,))
     back_codes = adapter_scale * sum_pairs(
         jnp.concatenate([nt(d_gate, gate_b), nt(d_up, up_b)], axis=1)
     )
     back_codes = back_codes.astype(jnp.bfloat16)
     back_gate, back_up = back_codes[:, :rank], back_codes[:, rank:]
-    dx_back = send_back(dx_kept, dx_chip, nt(back_gate, gate_a) + nt(back_up, up_a))
+    dx_extra = nt(back_gate, gate_a) + nt(back_up, up_a)
+    out_back = stack_rows(out_back, order, (dx_chip,))
+    dx_back = jnp.concatenate(send_back(dx_kept, meet(dx_chip), dx_extra, dx_kept))
 
     grad_codes = contract_matrices(x_part, back_codes, 0, 0)
     grad_list = (

time: 274 us -> 265 us (0.967); the launches traced: 273 us -> 261 us
  starting transfers between devices: 81.7 us -> 48.9 us
  Pallas kernels: 101 us -> 114 us
  waiting for transfers between devices: 63.6 us -> 69.9 us
    ppermute x12, starting transfers between devices: 53.1 us -> 25.6 us  [rotate(): lax.ppermute(arr, 'expert', [(e, (e + shift) % experts) for e in range(ex...]
    pallas_call x10 -> x22, Pallas kernels: 101 us -> 114 us  [call_tiles(): pl.pallas_call(inner, grid_spec=pltpu.PrefetchScalarGridSpec(num_scalar_p...]
    ppermute x12, waiting for transfers between devices: 22 us -> 31.2 us  [rotate(): lax.ppermute(arr, 'expert', [(e, (e + shift) % experts) for e in range(ex...]
    ppermute x34 -> x35, starting transfers between devices: 28.6 us -> 23.3 us  [swap(): return lax.ppermute(arr, axis, [(0, 1), (1, 0)])]
    ppermute x34 -> x35, waiting for transfers between devices: 41.7 us -> 38.7 us  [swap(): return lax.ppermute(arr, axis, [(0, 1), (1, 0)])]
    dot_general x20 -> x23, matrix products: 16.9 us -> 16.8 us  [contract_matrices(): lax.dot_general(left_op, right_op, (((left_dim,), (right_dim,)), ((), ())...]
  transfers between devices with their start and end apart: 46 -> 47, of which waited for: 17 -> 14; matrix products, arithmetic and copies ran while one was open for 6% -> 8% of each run, Pallas kernels for 24% -> 43%
where the time goes in v2:
time: 265 us; the launch traced here: 261 us
  Pallas kernels  114 us (43%)
  waiting for transfers between devices  69.9 us (26%)
  starting transfers between devices  48.9 us (18%)
  matrix products  16.8 us (6%)
  local copies, waits for them, and re-layouts  6.98 us (3%)
  other arithmetic  2.76 us (1%)
    pallas_call x22, Pallas kernels, call_tiles(): pl.pallas_call(inner, grid_spec=pltpu.PrefetchScalarGridSpec(num_scalar_p...  114 us
    ppermute x35, waiting for transfers between devices, swap(): return lax.ppermute(arr, axis, [(0, 1), (1, 0)])  38.7 us
    ppermute x12, waiting for transfers between devices, rotate(): lax.ppermute(arr, 'expert', [(e, (e + shift) % experts) for e in range(ex...  31.2 us
    ppermute x12, starting transfers between devices, rotate(): lax.ppermute(arr, 'expert', [(e, (e + shift) % experts) for e in range(ex...  25.6 us
    ppermute x35, starting transfers between devices, swap(): return lax.ppermute(arr, axis, [(0, 1), (1, 0)])  23.3 us
    dot_general x23, matrix products, contract_matrices(): lax.dot_general(left_op, right_op, (((left_dim,), (right_dim,)), ((), ())...  16.8 us
  transfers between devices with their start and end apart: 47, of which 14 were waited for; matrix products, arithmetic and copies ran while one was open for 8% of the time, Pallas kernels for 43%

profile of v2, /device:TPU:0, one launch (start us, length us, event | category | flops | bytes accessed | tf_op | source)
XLA Modules:
  0.0 260.7 jit_solution(3858730783513467874)
XLA Ops:
  1.8 3.0 %collective-permute-start.10 = (bf16[1536,128]{0,1:T(8,128)(2,1)S(1)}, bf16[1536,128]{0,1:T(8,128)(2,1)S(1)}, u32[]{:S(2)}, u32[]{:S(2)}) collective-permute-start(bf16[1536,128]{0,1:T(8,128)(2,1)S(1)} %pad_maximum_fusion.1), channel_id=1, source_target_pairs={{0,8},{8,0},{1,9},{9,1},{2,10},{10,2},{3,11},{11,3},{4,12},{12,4},... | collective-permute-start | bytes 1179656 | tf_op jit(solution)/shard_map/ppermute | solution.py:297
  7.9 3.6 %collective-permute-start.2 = (bf16[80,1536]{1,0:T(8,128)(2,1)}, bf16[80,1536]{1,0:T(8,128)(2,1)S(1)}, u32[]{:S(2)}, u32[]{:S(2)}) collective-permute-start(bf16[80,1536]{1,0:T(8,128)(2,1)} %get-tuple-element.47), channel_id=1, source_target_pairs={{0,6},{2,0},{4,2},{6,4},{1,7},{3,1},{5,3},{7,5},{8,14},{10,8},{12,... | collective-permute-start | bytes 737288 | tf_op jit(solution)/shard_map/ppermute | solution.py:308
  14.1 4.1 %collective-permute-done.2.refs_4_ = bf16[80,1536]{1,0:T(8,128)(2,1)S(1)} collective-permute-done((bf16[80,1536]{1,0:T(8,128)(2,1)}, bf16[80,1536]{1,0:T(8,128)(2,1)S(1)}, u32[]{:S(2)}, u32[]{:S(2)}) %collective-permute-start.2) | collective-permute-done | bytes 245792 | tf_op jit(solution)/shard_map/ppermute | solution.py:308
  18.7 10.4 %collective-permute-done.refs_2_ = bf16[80,1536]{1,0:T(8,128)(2,1)S(1)} collective-permute-done((bf16[80,1536]{1,0:T(8,128)(2,1)}, bf16[80,1536]{1,0:T(8,128)(2,1)S(1)}, u32[]{:S(2)}, u32[]{:S(2)}) %collective-permute-start) | collective-permute-done | bytes 245792 | tf_op jit(solution)/shard_map/ppermute | solution.py:308
  29.7 3.6 %collective-permute-done.1.refs_3_ = bf16[80,1536]{1,0:T(8,128)(2,1)S(1)} collective-permute-done((bf16[80,1536]{1,0:T(8,128)(2,1)S(1)}, bf16[80,1536]{1,0:T(8,128)(2,1)S(1)}, u32[]{:S(2)}, u32[]{:S(2)}) %collective-permute-start.1) | collective-permute-done | bytes 245792 | tf_op jit(solution)/shard_map/ppermute | solution.py:308
  37.3 5.0 %collective-permute-done.6 = bf16[80,1536]{1,0:T(8,128)(2,1)S(1)} collective-permute-done((bf16[80,1536]{1,0:T(8,128)(2,1)S(1)}, bf16[80,1536]{1,0:T(8,128)(2,1)S(1)}, u32[]{:S(2)}, u32[]{:S(2)}) %collective-permute-start.6) | collective-permute-done | bytes 245792 | tf_op jit(solution)/shard_map/ppermute | solution.py:297
  42.3 4.9 %collective-permute-done.7 = bf16[80,1536]{1,0:T(8,128)(2,1)S(1)} collective-permute-done((bf16[80,1536]{1,0:T(8,128)(2,1)S(1)}, bf16[80,1536]{1,0:T(8,128)(2,1)S(1)}, u32[]{:S(2)}, u32[]{:S(2)}) %collective-permute-start.7) | collective-permute-done | bytes 245792 | tf_op jit(solution)/shard_map/ppermute | solution.py:297
  47.4 4.7 %collective-permute-start.12 = (bf16[80,1536]{1,0:T(8,128)(2,1)S(1)}, bf16[80,1536]{1,0:T(8,128)(2,1)S(1)}, u32[]{:S(2)}, u32[]{:S(2)}) collective-permute-start(bf16[80,1536]{1,0:T(8,128)(2,1)S(1)} %get-tuple-element.44), channel_id=1, source_target_pairs={{0,2},{2,4},{4,6},{6,0},{1,3},{3,5},{5,7},{7,1},{8,10},{10,12},{12... | collective-permute-start | bytes 737288 | tf_op jit(solution)/shard_map/ppermute | solution.py:308
  54.5 2.9 %collective-permute-start.14 = (bf16[80,1536]{1,0:T(8,128)(2,1)S(1)}, bf16[80,1536]{1,0:T(8,128)(2,1)S(1)}, u32[]{:S(2)}, u32[]{:S(2)}) collective-permute-start(bf16[80,1536]{1,0:T(8,128)(2,1)S(1)} %get-tuple-element.42), channel_id=1, source_target_pairs={{0,6},{2,0},{4,2},{6,4},{1,7},{3,1},{5,3},{7,5},{8,14},{10,8},{12,... | collective-permute-start | bytes 737288 | tf_op jit(solution)/shard_map/ppermute | solution.py:308
  59.8 14.9 %shard_map.196 = (bf16[320,2048]{1,0:T(8,128)(2,1)S(1)}, f32[320,2048]{1,0:T(8,128)}, f32[320,2048]{1,0:T(8,128)}) custom-call(s32[4]{0:T(128)S(1)} %pad_add_fusion.order_ref, bf16[320,1536]{1,0:T(8,128)(2,1)S(1)} %pad_maximum_fusion.refs_0_, bf16[320,1536]{1,0:T(8,128)(2,1)S(1)} %collective-permute-done.3.refs_1_, ...), custom_call_target="tpu_custom_call" | custom-call | flops 8053063680 | bytes 25165824 | tf_op jit(solution)/shard_map/pallas_call | solution.py:119
  76.9 14.9 %shard_map.199 = (bf16[320,2048]{1,0:T(8,128)(2,1)}, f32[320,2048]{1,0:T(8,128)}, f32[320,2048]{1,0:T(8,128)}) custom-call(s32[4]{0:T(128)S(1)} %pad_add_fusion.order_ref, bf16[320,1536]{1,0:T(8,128)(2,1)S(1)} %pad_maximum_fusion.refs_0_, ...), custom_call_target="tpu_custom_call", output_to_operand_aliasing={{0}: (17, {}), {1}: (18, {}), {2}: (19, {})} | custom-call | flops 8053063680 | bytes 25165824 | tf_op jit(solution)/shard_map/pallas_call | solution.py:119
  101.4 16.9 %collective-permute-done.26 = f32[320,64]{0,1:T(8,128)S(1)} collective-permute-done((f32[320,64]{0,1:T(8,128)S(1)}, f32[320,64]{0,1:T(8,128)S(1)}, u32[]{:S(2)}, u32[]{:S(2)}) %collective-permute-start.26) | collective-permute-done | bytes 81952 | tf_op jit(solution)/shard_map/ppermute | solution.py:297
  119.0 6.9 %collective-permute-done.18 = bf16[80,1536]{1,0:T(8,128)(2,1)S(1)} collective-permute-done((bf16[80,1536]{1,0:T(8,128)(2,1)S(1)}, bf16[80,1536]{1,0:T(8,128)(2,1)S(1)}, u32[]{:S(2)}, u32[]{:S(2)}) %collective-permute-start.18) | collective-permute-done | bytes 245792 | tf_op jit(solution)/shard_map/ppermute | solution.py:297
  127.6 5.5 %shard_map.200.refs_2_ = bf16[320,1536]{1,0:T(8,128)(2,1)S(1)} custom-call(s32[4]{0:T(128)S(1)} %pad_add_fusion.order_ref, bf16[320,2048]{1,0:T(8,128)(2,1)S(1)} %copy-done.3, bf16[2048,6144]{1,0:T(8,128)(2,1)} %bitcast.114, bf16[320,1536]{1,0:T(8,128)(2,1)S(1)} %constant_dynamic-update-slice_fusion.4.refs_2_), custom_call_target="tpu_custom_call" | custom-call | flops 2013265920 | bytes 6291456 | tf_op jit(solution)/shard_map/pallas_call | solution.py:119
  134.8 5.5 %shard_map.201.refs_12_ = bf16[320,1536]{1,0:T(8,128)(2,1)S(1)} custom-call(s32[4]{0:T(128)S(1)} %pad_add_fusion.order_ref, bf16[320,2048]{1,0:T(8,128)(2,1)S(1)} %copy-done.3, bf16[2048,6144]{1,0:T(8,128)(2,1)} %bitcast.115, bf16[320,1536]{1,0:T(8,128)(2,1)S(1)} %shard_map.200.refs_2_), custom_call_target="tpu_custom_call" | custom-call | flops 2013265920 | bytes 6291456 | tf_op jit(solution)/shard_map/pallas_call | solution.py:119
  140.4 16.7 %shard_map.202 = (bf16[320,2048]{1,0:T(8,128)(2,1)}, bf16[320,2048]{1,0:T(8,128)(2,1)}) custom-call(s32[4]{0:T(128)S(1)} %pad_add_fusion.order_ref, bf16[320,1536]{1,0:T(8,128)(2,1)S(1)} %shard_map.198.refs_19_.refs_0_, bf16[320,1536]{1,0:T(8,128)(2,1)S(1)} %collective-permute-done.21.refs_1_, ...), custom_call_target="tpu_custom_call" | custom-call | flops 8053063680 | bytes 25165824 | tf_op jit(solution)/shard_map/pallas_call | solution.py:119
  158.4 5.5 %shard_map.203.refs_3_ = bf16[320,1536]{1,0:T(8,128)(2,1)S(1)} custom-call(s32[4]{0:T(128)S(1)} %pad_add_fusion.order_ref, bf16[320,2048]{1,0:T(8,128)(2,1)S(1)} %copy-done.3, bf16[2048,6144]{1,0:T(8,128)(2,1)} %bitcast.120, bf16[320,1536]{1,0:T(8,128)(2,1)S(1)} %collective-permute-done.20.refs_2_, bf16[320,2048]{1,0:T(8,128)(2,1)S(1)} %copy-done.5), custom_call_target="tpu_custom_call" | custom-call | flops 2013265920 | bytes 6291456 | tf_op jit(solution)/shard_map/pallas_call | solution.py:119
  169.2 5.6 %shard_map.204.refs_4_.refs_0_ = f32[320,1536]{1,0:T(8,128)S(1)} custom-call(s32[4]{0:T(128)S(1)} %pad_add_fusion.order_ref, bf16[320,2048]{1,0:T(8,128)(2,1)S(1)} %copy-done.3, bf16[2048,6144]{1,0:T(8,128)(2,1)} %bitcast.121, bf16[320,1536]{1,0:T(8,128)(2,1)S(1)} %collective-permute-done.19.refs_2_, bf16[320,1536]{1,0:T(8,128)(2,1)S(1)} %shard_map.203.refs_3_), custom_call_target="tpu_custom_call" | custom-call | flops 2013265920 | bytes 6291456 | tf_op jit(solution)/shard_map/pallas_call | solution.py:119
  174.8 9.2 %shard_map.205.refs_3_.refs_4_ = bf16[320,1536]{1,0:T(8,128)(2,1)S(1)} custom-call(s32[4]{0:T(128)S(1)} %pad_add_fusion.order_ref, bf16[320,2048]{1,0:T(8,128)(2,1)S(1)} %copy-done.5, bf16[320,2048]{1,0:T(8,128)(2,1)S(1)} %copy-done.7, bf16[6144,2048]{1,0:T(8,128)(2,1)} %bitcast.98, bf16[6144,2048]{1,0:T(8,128)(2,1)} %bitcast.110, ...), custom_call_target="tpu_custom_call" | custom-call | flops 4026531840 | bytes 12582912 | tf_op jit(solution)/shard_map/pallas_call | solution.py:119
  184.0 9.4 %shard_map.210.refs_5_ = bf16[320,1536]{1,0:T(8,128)(2,1)S(1)} custom-call(s32[4]{0:T(128)S(1)} %pad_add_fusion.order_ref, bf16[320,2048]{1,0:T(8,128)(2,1)S(1)} %copy-done.5, bf16[320,2048]{1,0:T(8,128)(2,1)S(1)} %copy-done.7, bf16[6144,2048]{1,0:T(8,128)(2,1)} %bitcast.99, bf16[6144,2048]{1,0:T(8,128)(2,1)} %bitcast.111, ...), custom_call_target="tpu_custom_call" | custom-call | flops 4026531840 | bytes 12582912 | tf_op jit(solution)/shard_map/pallas_call | solution.py:119
  204.8 9.6 %shard_map.211.refs_4_.refs_5_ = bf16[320,1536]{1,0:T(8,128)(2,1)S(1)} custom-call(s32[4]{0:T(128)S(1)} %pad_add_fusion.order_ref, bf16[320,2048]{1,0:T(8,128)(2,1)S(1)} %copy-done.5, bf16[320,2048]{1,0:T(8,128)(2,1)} %get-tuple-element.24.refs_1_, bf16[6144,2048]{1,0:T(8,128)(2,1)} %bitcast.100, bf16[6144,2048]{1,0:T(8,128)(2,1)} %bitcast.112, ...), custom_call_target="tpu_custom_call" | custom-call | flops 4026531840 | bytes 12582912 | tf_op jit(solution)/shard_map/pallas_call | solution.py:119
  224.9 10.2 %shard_map.213.refs_0_.refs_3_ = f32[320,1536]{1,0:T(8,128)} custom-call(s32[4]{0:T(128)S(1)} %pad_add_fusion.order_ref, bf16[320,2048]{1,0:T(8,128)(2,1)S(1)} %copy-done.6, bf16[320,2048]{1,0:T(8,128)(2,1)S(1)} %copy-done.8, bf16[6144,2048]{1,0:T(8,128)(2,1)} %bitcast.101, bf16[6144,2048]{1,0:T(8,128)(2,1)} %bitcast.113, ...), custom_call_target="tpu_custom_call" | custom-call | flops 4026531840 | bytes 12582912 | tf_op jit(solution)/shard_map/pallas_call | solution.py:119
  237.9 4.1 %collective-permute-start.43 = (bf16[80,1536]{1,0:T(8,128)(2,1)S(1)}, bf16[80,1536]{1,0:T(8,128)(2,1)S(1)}, u32[]{:S(2)}, u32[]{:S(2)}) collective-permute-start(bf16[80,1536]{1,0:T(8,128)(2,1)S(1)} %shard_map.214.refs_3_), channel_id=1, source_target_pairs={{0,4},{2,6},{4,0},{6,2},{1,5},{3,7},{5,1},{7,3},{8,12},{10,14},{12... | collective-permute-start | bytes 737288 | tf_op jit(solution)/shard_map/ppermute | solution.py:308
  249.3 8.3 %collective-permute-done.44 = bf16[80,1536]{1,0:T(8,128)(2,1)S(1)} collective-permute-done((bf16[80,1536]{1,0:T(8,128)(2,1)S(1)}, bf16[80,1536]{1,0:T(8,128)(2,1)S(1)}, u32[]{:S(2)}, u32[]{:S(2)}) %collective-permute-start.44) | collective-permute-done | bytes 245792 | tf_op jit(solution)/shard_map/ppermute | solution.py:308
  (207 shorter events, 73.4 us)
Async XLA Ops:
  1.8 50.4 %collective-permute-start.10 = (bf16[1536,128]{0,1:T(8,128)(2,1)S(1)}, bf16[1536,128]{0,1:T(8,128)(2,1)S(1)}, u32[]{:S(2)}, u32[]{:S(2)}) collective-permute-start(bf16[1536,128]{0,1:T(8,128)(2,1)S(1)} %pad_maximum_fusion.1), channel_id=1, source_target_pairs={{0,8},{8,0},{1,9},{9,1},{2,10},{10,2},{3,11},{11,3},{4,12},{12,4},... | collective-permute-start | bytes 1179656 | tf_op jit(solution)/shard_map/ppermute | solution.py:297
  4.8 49.7 %collective-permute-start.9 = (bf16[1536,128]{0,1:T(8,128)(2,1)S(1)}, bf16[1536,128]{0,1:T(8,128)(2,1)}, u32[]{:S(2)}, u32[]{:S(2)}) collective-permute-start(bf16[1536,128]{0,1:T(8,128)(2,1)S(1)} %pad_maximum_fusion.1), channel_id=1, source_target_pairs={{0,1},{1,0},{2,3},{3,2},{4,5},{5,4},{6,7},{7,6},{8,9},{9,8},{10,11... | collective-permute-start | bytes 1179656 | tf_op jit(solution)/shard_map/ppermute | solution.py:297
  11.5 21.8 %collective-permute-start.1 = (bf16[80,1536]{1,0:T(8,128)(2,1)S(1)}, bf16[80,1536]{1,0:T(8,128)(2,1)S(1)}, u32[]{:S(2)}, u32[]{:S(2)}) collective-permute-start(bf16[80,1536]{1,0:T(8,128)(2,1)S(1)} %get-tuple-element.48), channel_id=1, source_target_pairs={{0,4},{2,6},{4,0},{6,2},{1,5},{3,7},{5,1},{7,3},{8,12},{10,14},{12... | collective-permute-start | bytes 737288 | tf_op jit(solution)/shard_map/ppermute | solution.py:308
  33.4 24.0 %collective-permute-start.3 = (bf16[320,1536]{1,0:T(8,128)(2,1)S(1)}, bf16[320,1536]{1,0:T(8,128)(2,1)S(1)}, u32[]{:S(2)}, u32[]{:S(2)}) collective-permute-start(bf16[320,1536]{1,0:T(8,128)(2,1)S(1)} %pad_maximum_fusion.refs_0_), channel_id=1, source_target_pairs={{0,1},{1,0},{2,3},{3,2},{4,5},{5,4},{6,7},{7,6},{8,9},{9,8},{10,11... | collective-permute-start | bytes 2949128 | tf_op jit(solution)/shard_map/ppermute | solution.py:297
  47.4 27.4 %collective-permute-start.12 = (bf16[80,1536]{1,0:T(8,128)(2,1)S(1)}, bf16[80,1536]{1,0:T(8,128)(2,1)S(1)}, u32[]{:S(2)}, u32[]{:S(2)}) collective-permute-start(bf16[80,1536]{1,0:T(8,128)(2,1)S(1)} %get-tuple-element.44), channel_id=1, source_target_pairs={{0,2},{2,4},{4,6},{6,0},{1,3},{3,5},{5,7},{7,1},{8,10},{10,12},{12... | collective-permute-start | bytes 737288 | tf_op jit(solution)/shard_map/ppermute | solution.py:308
  52.1 22.6 %collective-permute-start.13 = (bf16[80,1536]{1,0:T(8,128)(2,1)S(1)}, bf16[80,1536]{1,0:T(8,128)(2,1)S(1)}, u32[]{:S(2)}, u32[]{:S(2)}) collective-permute-start(bf16[80,1536]{1,0:T(8,128)(2,1)S(1)} %get-tuple-element.43), channel_id=1, source_target_pairs={{0,4},{2,6},{4,0},{6,2},{1,5},{3,7},{5,1},{7,3},{8,12},{10,14},{12... | collective-permute-start | bytes 737288 | tf_op jit(solution)/shard_map/ppermute | solution.py:308
  54.5 20.3 %collective-permute-start.14 = (bf16[80,1536]{1,0:T(8,128)(2,1)S(1)}, bf16[80,1536]{1,0:T(8,128)(2,1)S(1)}, u32[]{:S(2)}, u32[]{:S(2)}) collective-permute-start(bf16[80,1536]{1,0:T(8,128)(2,1)S(1)} %get-tuple-element.42), channel_id=1, source_target_pairs={{0,6},{2,0},{4,2},{6,4},{1,7},{3,1},{5,3},{7,5},{8,14},{10,8},{12,... | collective-permute-start | bytes 737288 | tf_op jit(solution)/shard_map/ppermute | solution.py:308
  94.4 46.0 %collective-permute-start.21 = (bf16[320,1536]{1,0:T(8,128)(2,1)S(1)}, bf16[320,1536]{1,0:T(8,128)(2,1)S(1)}, u32[]{:S(2)}, u32[]{:S(2)}) collective-permute-start(bf16[320,1536]{1,0:T(8,128)(2,1)S(1)} %shard_map.198.refs_19_.refs_0_), channel_id=1, source_target_pairs={{0,1},{1,0},{2,3},{3,2},{4,5},{5,4},{6,7},{7,6},{8,9},{9,8},{10,11... | collective-permute-start | bytes 2949128 | tf_op jit(solution)/shard_map/ppermute | solution.py:297
  94.7 24.2 %collective-permute-start.15 = (bf16[80,1536]{1,0:T(8,128)(2,1)S(1)}, bf16[80,1536]{1,0:T(8,128)(2,1)S(1)}, u32[]{:S(2)}, u32[]{:S(2)}) collective-permute-start(bf16[80,1536]{1,0:T(8,128)(2,1)S(1)} %get-tuple-element.41), channel_id=1, source_target_pairs={{0,8},{8,0},{1,9},{9,1},{2,10},{10,2},{3,11},{11,3},{4,12},{12,4},... | collective-permute-start | bytes 737288 | tf_op jit(solution)/shard_map/ppermute | solution.py:297
  96.2 22.7 %collective-permute-start.16 = (bf16[80,1536]{1,0:T(8,128)(2,1)S(1)}, bf16[80,1536]{1,0:T(8,128)(2,1)S(1)}, u32[]{:S(2)}, u32[]{:S(2)}) collective-permute-start(bf16[80,1536]{1,0:T(8,128)(2,1)S(1)} %get-tuple-element.40), channel_id=1, source_target_pairs={{0,8},{8,0},{1,9},{9,1},{2,10},{10,2},{3,11},{11,3},{4,12},{12,4},... | collective-permute-start | bytes 737288 | tf_op jit(solution)/shard_map/ppermute | solution.py:297
  96.7 22.2 %collective-permute-start.17 = (bf16[80,1536]{1,0:T(8,128)(2,1)S(1)}, bf16[80,1536]{1,0:T(8,128)(2,1)S(1)}, u32[]{:S(2)}, u32[]{:S(2)}) collective-permute-start(bf16[80,1536]{1,0:T(8,128)(2,1)S(1)} %get-tuple-element.39), channel_id=1, source_target_pairs={{0,8},{8,0},{1,9},{9,1},{2,10},{10,2},{3,11},{11,3},{4,12},{12,4},... | collective-permute-start | bytes 737288 | tf_op jit(solution)/shard_map/ppermute | solution.py:297
  133.2 23.9 %collective-permute-start.20 = (bf16[320,1536]{1,0:T(8,128)(2,1)S(1)}, bf16[320,1536]{1,0:T(8,128)(2,1)S(1)}, u32[]{:S(2)}, u32[]{:S(2)}) collective-permute-start(bf16[320,1536]{1,0:T(8,128)(2,1)S(1)} %shard_map.200.refs_2_), channel_id=1, source_target_pairs={{0,1},{1,0},{2,3},{3,2},{4,5},{5,4},{6,7},{7,6},{8,9},{9,8},{10,11... | collective-permute-start | bytes 2949128 | tf_op jit(solution)/shard_map/ppermute | solution.py:297
  140.3 28.9 %collective-permute-start.19 = (bf16[320,1536]{1,0:T(8,128)(2,1)S(1)}, bf16[320,1536]{1,0:T(8,128)(2,1)S(1)}, u32[]{:S(2)}, u32[]{:S(2)}) collective-permute-start(bf16[320,1536]{1,0:T(8,128)(2,1)S(1)} %shard_map.201.refs_12_), channel_id=1, source_target_pairs={{0,1},{1,0},{2,3},{3,2},{4,5},{5,4},{6,7},{7,6},{8,9},{9,8},{10,11... | collective-permute-start | bytes 2949128 | tf_op jit(solution)/shard_map/ppermute | solution.py:297
  164.0 35.3 %collective-permute-start.27 = (bf16[80,1536]{1,0:T(8,128)(2,1)S(1)}, bf16[80,1536]{1,0:T(8,128)(2,1)S(1)}, u32[]{:S(2)}, u32[]{:S(2)}) collective-permute-start(bf16[80,1536]{1,0:T(8,128)(2,1)S(1)} %get-tuple-element.37), channel_id=1, source_target_pairs={{0,8},{8,0},{1,9},{9,1},{2,10},{10,2},{3,11},{11,3},{4,12},{12,4},... | collective-permute-start | bytes 737288 | tf_op jit(solution)/shard_map/ppermute | solution.py:297
  164.6 34.0 %collective-permute-start.28 = (bf16[80,1536]{1,0:T(8,128)(2,1)S(1)}, bf16[80,1536]{1,0:T(8,128)(2,1)S(1)}, u32[]{:S(2)}, u32[]{:S(2)}) collective-permute-start(bf16[80,1536]{1,0:T(8,128)(2,1)S(1)} %get-tuple-element.36), channel_id=1, source_target_pairs={{0,8},{8,0},{1,9},{9,1},{2,10},{10,2},{3,11},{11,3},{4,12},{12,4},... | collective-permute-start | bytes 737288 | tf_op jit(solution)/shard_map/ppermute | solution.py:297
  166.1 31.3 %collective-permute-start.29 = (bf16[80,1536]{1,0:T(8,128)(2,1)S(1)}, bf16[80,1536]{1,0:T(8,128)(2,1)S(1)}, u32[]{:S(2)}, u32[]{:S(2)}) collective-permute-start(bf16[80,1536]{1,0:T(8,128)(2,1)S(1)} %get-tuple-element.35), channel_id=1, source_target_pairs={{0,8},{8,0},{1,9},{9,1},{2,10},{10,2},{3,11},{11,3},{4,12},{12,4},... | collective-permute-start | bytes 737288 | tf_op jit(solution)/shard_map/ppermute | solution.py:297
  166.7 30.2 %collective-permute-start.30 = (bf16[80,1536]{1,0:T(8,128)(2,1)S(1)}, bf16[80,1536]{1,0:T(8,128)(2,1)S(1)}, u32[]{:S(2)}, u32[]{:S(2)}) collective-permute-start(bf16[80,1536]{1,0:T(8,128)(2,1)S(1)} %get-tuple-element.34), channel_id=1, source_target_pairs={{0,8},{8,0},{1,9},{9,1},{2,10},{10,2},{3,11},{11,3},{4,12},{12,4},... | collective-permute-start | bytes 737288 | tf_op jit(solution)/shard_map/ppermute | solution.py:297
  197.5 27.4 %collective-permute-start.35 = (bf16[320,1536]{1,0:T(8,128)(2,1)S(1)}, bf16[320,1536]{1,0:T(8,128)(2,1)S(1)}, u32[]{:S(2)}, u32[]{:S(2)}) collective-permute-start(bf16[320,1536]{1,0:T(8,128)(2,1)S(1)} %shard_map.210.refs_5_), channel_id=1, source_target_pairs={{0,1},{1,0},{2,3},{3,2},{4,5},{5,4},{6,7},{7,6},{8,9},{9,8},{10,11... | collective-permute-start | bytes 2949128 | tf_op jit(solution)/shard_map/ppermute | solution.py:297
  198.7 21.7 %collective-permute-start.32 = (bf16[80,1536]{1,0:T(8,128)(2,1)S(1)}, bf16[80,1536]{1,0:T(8,128)(2,1)S(1)}, u32[]{:S(2)}, u32[]{:S(2)}) collective-permute-start(bf16[80,1536]{1,0:T(8,128)(2,1)S(1)} %shard_map.206.refs_3_), channel_id=1, source_target_pairs={{0,4},{2,6},{4,0},{6,2},{1,5},{3,7},{5,1},{7,3},{8,12},{10,14},{12... | collective-permute-start | bytes 737288 | tf_op jit(solution)/shard_map/ppermute | solution.py:308
  199.4 19.5 %collective-permute-start.31 = (bf16[80,1536]{1,0:T(8,128)(2,1)S(1)}, bf16[80,1536]{1,0:T(8,128)(2,1)S(1)}, u32[]{:S(2)}, u32[]{:S(2)}) collective-permute-start(bf16[80,1536]{1,0:T(8,128)(2,1)S(1)} %shard_map.208.refs_3_), channel_id=1, source_target_pairs={{0,6},{2,0},{4,2},{6,4},{1,7},{3,1},{5,3},{7,5},{8,14},{10,8},{12,... | collective-permute-start | bytes 737288 | tf_op jit(solution)/shard_map/ppermute | solution.py:308
  214.5 27.5 %collective-permute-start.40 = (bf16[80,1536]{1,0:T(8,128)(2,1)S(1)}, bf16[80,1536]{1,0:T(8,128)(2,1)S(1)}, u32[]{:S(2)}, u32[]{:S(2)}) collective-permute-start(bf16[80,1536]{1,0:T(8,128)(2,1)S(1)} %get-tuple-element.32), channel_id=1, source_target_pairs={{0,8},{8,0},{1,9},{9,1},{2,10},{10,2},{3,11},{11,3},{4,12},{12,4},... | collective-permute-start | bytes 737288 | tf_op jit(solution)/shard_map/ppermute | solution.py:297
  220.4 23.3 %collective-permute-start.39 = (bf16[80,1536]{1,0:T(8,128)(2,1)S(1)}, bf16[80,1536]{1,0:T(8,128)(2,1)S(1)}, u32[]{:S(2)}, u32[]{:S(2)}) collective-permute-start(bf16[80,1536]{1,0:T(8,128)(2,1)S(1)} %get-tuple-element.33), channel_id=1, source_target_pairs={{0,8},{8,0},{1,9},{9,1},{2,10},{10,2},{3,11},{11,3},{4,12},{12,4},... | collective-permute-start | bytes 737288 | tf_op jit(solution)/shard_map/ppermute | solution.py:297
  220.9 27.7 %collective-permute-start.38 = (bf16[80,1536]{1,0:T(8,128)(2,1)S(1)}, bf16[80,1536]{1,0:T(8,128)(2,1)S(1)}, u32[]{:S(2)}, u32[]{:S(2)}) collective-permute-start(bf16[80,1536]{1,0:T(8,128)(2,1)S(1)} %get-tuple-element.30), channel_id=1, source_target_pairs={{0,8},{8,0},{1,9},{9,1},{2,10},{10,2},{3,11},{11,3},{4,12},{12,4},... | collective-permute-start | bytes 737288 | tf_op jit(solution)/shard_map/ppermute | solution.py:297
  237.9 21.4 %collective-permute-start.43 = (bf16[80,1536]{1,0:T(8,128)(2,1)S(1)}, bf16[80,1536]{1,0:T(8,128)(2,1)S(1)}, u32[]{:S(2)}, u32[]{:S(2)}) collective-permute-start(bf16[80,1536]{1,0:T(8,128)(2,1)S(1)} %shard_map.214.refs_3_), channel_id=1, source_target_pairs={{0,4},{2,6},{4,0},{6,2},{1,5},{3,7},{5,1},{7,3},{8,12},{10,14},{12... | collective-permute-start | bytes 737288 | tf_op jit(solution)/shard_map/ppermute | solution.py:308
  (53 other events, 437.7 us)
